TPU v7x, 512 devices: a whole 4x8x8 slice. The times are simulated.
512 devices in a mesh: row: 32 (over y, z_lo, core), col: 16 (over x, z_hi).
Axes of the slice: x: 4, y: 8, z: 8 (z_hi: 4, z_lo: 2; z = z_hi * 2 + z_lo), core: 2. Of those that a mesh axis runs over, the one named last changes fastest.
Arguments:
- start_amps: float32 [4096, 4096], P('row', 'col'), may hold values from -1.75 to 1.75
- exchange_ints: bfloat16 [4096, 4096], P('row', 'col'), may hold values from -6 to 6
- fitted_ints: bfloat16 [4096, 24576], P('col', 'row'), may hold values from -0.25 to 0.25
- pao_energy: float32 [2048], replicated, may hold values from 0.3 to 3
- occ_fock: float32 [8, 8], replicated, may hold values from -1.5 to 0.6, as said below
- domains: int32 [8, 512], replicated, may hold values from 0 to 2047, as said below
- pair_list: int32 [36, 2], replicated, may hold values from 0 to 7, as said below
Outputs:
- sym_amps: float32 [4096, 4096], P('row', 'col')
- gamma: bfloat16 [4096, 24576], P('col', 'row')
Inputs may be any that keep to these rules, and one draw needn't show every extreme that they name: `pair_list`: each row is an ordered pair (I, J) of orbitals. Every (I, I) is listed; when (I, J) is listed so is (J, I); no pair is listed twice; 14 unordered pairs of distinct orbitals are listed. `domains`: each row holds 512 distinct PAO indices. `occ_fock`: Symmetric; its diagonal lies between -1.5 and -0.4.
All inputs are finite; a program needn't handle non-finite values.
Results may differ from a plain program's by a relative error of at most 0.001.
The roundings to bfloat16 on the way count: a program that leaves them out, or rounds other values in their place, can miss the bound.
Values may be sent and summed in bfloat16 or wider, within the bound.
A program may use at most 64 MiB of HBM per device.

v0:
```python
import jax
import jax.numpy as jnp
from jax import lax
from jax.sharding import PartitionSpec as P

ITERS = 2


full_precision = lax.Precision.HIGHEST


def swapped(block, axis, apart):
    count = lax.axis_size(axis)
    route = []
    for low in range(count):
        high = low | 1 << apart
        if high != low and high < count:
            route += [(low, high), (high, low)]
    return lax.ppermute(block, axis, route)


def lookup(values_table, indices):
    extent = values_table.shape[0]
    matches = indices[:, None] == jnp.arange(extent, dtype=jnp.int32)[None, :]
    return jnp.sum(jnp.where(matches, values_table[None, :], 0.0), axis=1)


def pair_mask(pair_list, norbit):
    orbits = jnp.arange(norbit, dtype=jnp.int32)
    first_hot = (pair_list[:, 0][:, None] == orbits[None, :]).astype(jnp.float32)
    second_hot = (pair_list[:, 1][:, None] == orbits[None, :]).astype(jnp.float32)
    return jnp.dot(first_hot.T, second_hot, precision=full_precision)


def placement(paos, domains, owners, fock_rows):
    norbit, width = domains.shape
    matches = paos[:, None, None] == domains[None, :, :]
    where_at = jnp.sum(
        jnp.where(matches, jnp.arange(width, dtype=jnp.int32)[None, None, :], 0), axis=2
    )
    present = jnp.any(matches, axis=2)
    orbits = jnp.arange(norbit, dtype=jnp.int32)
    position = orbits[None, :] * width + where_at
    weight = jnp.where(present & (owners[:, None] != orbits[None, :]), fock_rows, 0.0)
    return (position, weight)


def mirror_tile(current):
    tile_rows = current.shape[0]
    row_place = lax.axis_index("row")
    col_place = lax.axis_index("col")
    upper_half = row_place // 2
    parity = row_place % 2
    spread = jnp.bitwise_xor(upper_half, col_place)
    sections = lax.axis_size("col").bit_length() - 1
    moving = current
    for section_bit in range(sections):
        across = swapped(moving, "row", section_bit + 1)
        across = swapped(across, "col", section_bit)
        moving = jnp.where(jnp.right_shift(spread, section_bit) % 2 == 1, across, moving)
    keep_half = lax.dynamic_slice_in_dim(moving, parity * tile_rows, tile_rows, 1)
    send_half = lax.dynamic_slice_in_dim(moving, (1 - parity) * tile_rows, tile_rows, 1)
    other_half = swapped(send_half, "row", 0)
    lower_first = jnp.concatenate([keep_half.T, other_half.T], axis=1)
    upper_first = jnp.concatenate([other_half.T, keep_half.T], axis=1)
    return jnp.where(parity == 0, lower_first, upper_first)


def body(start_amps, exchange_ints, fitted_ints, pao_energy, occ_fock, domains, pair_list):
    tile_rows, tile_cols = start_amps.shape
    norbit, width = domains.shape
    row_start = lax.axis_index("row") * tile_rows
    col_start = lax.axis_index("col") * tile_cols
    listed = pair_mask(pair_list, norbit)
    orbits = jnp.arange(norbit, dtype=jnp.int32)
    row_owner = (row_start + jnp.arange(tile_rows, dtype=jnp.int32)) // width
    col_owner = (col_start + jnp.arange(tile_cols, dtype=jnp.int32)) // width
    row_picker = (row_owner[:, None] == orbits[None, :]).astype(jnp.float32)
    col_picker = (col_owner[:, None] == orbits[None, :]).astype(jnp.float32)
    flat_domains = domains.reshape(-1)
    row_paos = lax.dynamic_slice_in_dim(flat_domains, row_start, tile_rows)
    col_paos = lax.dynamic_slice_in_dim(flat_domains, col_start, tile_cols)
    fock_diagonal = jnp.diagonal(occ_fock)
    row_level = lookup(pao_energy, row_paos) - jnp.dot(
        row_picker, fock_diagonal, precision=full_precision
    )
    col_level = lookup(pao_energy, col_paos) - jnp.dot(
        col_picker, fock_diagonal, precision=full_precision
    )
    denominator = row_level[:, None] + col_level[None, :]
    tile_mask = jnp.dot(
        jnp.dot(row_picker, listed, precision=full_precision),
        col_picker.T,
        precision=full_precision,
    )
    row_position, row_weight = placement(
        row_paos, domains, row_owner, jnp.dot(row_picker, occ_fock, precision=full_precision)
    )
    col_position, col_weight = placement(
        col_paos, domains, col_owner, jnp.dot(col_picker, occ_fock, precision=full_precision)
    )
    exchange_full = exchange_ints.astype(jnp.float32)
    current = start_amps
    for sweep in range(ITERS):
        rounded = current.astype(jnp.bfloat16)
        column_panel = lax.all_gather(rounded, "row", axis=0, tiled=True)
        row_panel = lax.all_gather(rounded, "col", axis=1, tiled=True)
        picked_rows = jnp.take(column_panel, row_position, axis=0).astype(jnp.float32)
        left_term = jnp.einsum("rk,rkc->rc", row_weight, picked_rows, precision=full_precision)
        picked_cols = jnp.take(row_panel, col_position, axis=1).astype(jnp.float32)
        right_term = jnp.einsum("rck,ck->rc", picked_cols, col_weight, precision=full_precision)
        current = tile_mask * ((left_term + right_term - exchange_full) / denominator)
    mirrored = mirror_tile(current)
    sym_amps = 0.5 * (current + mirrored)
    sym_panel = lax.all_gather(sym_amps.astype(jnp.bfloat16), "row", axis=0, tiled=True)
    gamma_sum = lax.dot_general(
        sym_panel,
        lax.all_gather(fitted_ints, "col", axis=0, tiled=True),
        (((0,), (0,)), ((), ())),
        preferred_element_type=jnp.float32,
    )
    return (sym_amps, gamma_sum.astype(jnp.bfloat16))


def solution(mesh):
    return jax.shard_map(
        body,
        mesh=mesh,
        in_specs=(P("row", "col"), P("row", "col"), P("col", "row"), P(), P(), P(), P()),
        out_specs=(P("row", "col"), P("col", "row")),
        check_vma=False,
    )
```

profile of v0, /device:TPU:1, one launch (start us, length us, event | category | flops | bytes accessed | tf_op | source)
XLA Modules:
  0.0 469.3 jit_solution(15955946728502964013)
XLA Ops:
  10.4 6.2 %compare_reduce_fusion = pred[256,8]{1,0:T(8,128)(4,1)S(1)} fusion(s32[8,512]{1,0:T(8,128)} %param.16, s32[256]{0:T(256)S(1)} %dynamic_slice.13), kind=kLoop, calls=%fused_computation.6 | loop fusion | flops 2095104 | bytes 19456 | tf_op jit(solution)/shard_map/reduce_or | solution.py:41
  17.0 6.2 %fusion = s32[256,8]{1,0:T(8,128)S(1)} fusion(s32[8,512]{1,0:T(8,128)} %param.16, s32[256]{0:T(256)S(1)} %dynamic_slice.13), kind=kLoop, calls=%fused_computation.7 | loop fusion | flops 3143680 | bytes 25600 | tf_op jit(solution)/shard_map/reduce_sum | solution.py:38
  33.0 44.2 %all-gather.9.cloned.1.call-done = bf16[128,4096]{1,0:T(8,128)(2,1)} async-done(((bf16[128,256]{1,0:T(8,128)(2,1)}), bf16[128,4096]{1,0:T(8,128)(2,1)}) %all-gather.9.cloned.1.call-update) | async-done | bytes 1048592 | tf_op jit(solution)/shard_map/all_gather | solution.py:107
  78.8 6.2 %gather_fusion.2 = bf16[2048,128]{1,0:T(8,128)(2,1)S(1)} fusion(bf16[128,4096]{0,1:T(8,128)(2,1)S(1)} %copy.32, s32[2048]{0:T(1024)S(1)} %broadcast_clamp_fusion), kind=kCustom, calls=%fused_computation.1.clone | custom fusion | bytes 1056768 | tf_op jit(solution)/shard_map/jit(_take)/gather | solution.py:110
  86.6 58.2 %all-gather.7.cloned.1.call-done = bf16[4096,256]{1,0:T(8,128)(2,1)} async-done(((bf16[128,256]{1,0:T(8,128)(2,1)}), bf16[4096,256]{1,0:T(8,128)(2,1)}) %all-gather.7.cloned.1.call-update) | async-done | bytes 2097168 | tf_op jit(solution)/shard_map/all_gather | solution.py:106
  144.8 5.5 %gather_fusion.1 = bf16[1024,256]{1,0:T(8,128)(2,1)S(1)} fusion(bf16[4096,256]{1,0:T(8,128)(2,1)} %all-gather.7.cloned.1.call-done, s32[1024]{0:T(1024)S(1)} %broadcast_clamp_fusion.1), kind=kCustom, calls=%fused_computation.clone | custom fusion | bytes 1052672 | tf_op jit(solution)/shard_map/jit(_take)/gather | solution.py:108
  153.1 58.2 %all-gather.13.cloned.1.call-done = bf16[128,4096]{1,0:T(8,128)(2,1)} async-done(((bf16[128,256]{1,0:T(8,128)(2,1)}), bf16[128,4096]{1,0:T(8,128)(2,1)}) %all-gather.13.cloned.1.call-update) | async-done | bytes 1048592 | tf_op jit(solution)/shard_map/all_gather | solution.py:107
  213.0 6.2 %gather_fusion.4 = bf16[2048,128]{1,0:T(8,128)(2,1)S(1)} fusion(bf16[128,4096]{0,1:T(8,128)(2,1)S(1)} %copy.36, s32[2048]{0:T(1024)S(1)} %broadcast_clamp_fusion), kind=kCustom, calls=%fused_computation.3.clone | custom fusion | bytes 1056768 | tf_op jit(solution)/shard_map/jit(_take)/gather | solution.py:110
  220.7 58.1 %all-gather.11.cloned.1.call-done = bf16[4096,256]{1,0:T(8,128)(2,1)} async-done(((bf16[128,256]{1,0:T(8,128)(2,1)}), bf16[4096,256]{1,0:T(8,128)(2,1)}) %all-gather.11.cloned.1.call-update) | async-done | bytes 2097168 | tf_op jit(solution)/shard_map/all_gather | solution.py:106
  278.8 5.3 %gather_fusion.3 = bf16[1024,256]{1,0:T(8,128)(2,1)S(1)} fusion(bf16[4096,256]{1,0:T(8,128)(2,1)} %all-gather.11.cloned.1.call-done, s32[1024]{0:T(1024)S(1)} %broadcast_clamp_fusion.1), kind=kCustom, calls=%fused_computation.2.clone | custom fusion | bytes 1052672 | tf_op jit(solution)/shard_map/jit(_take)/gather | solution.py:108
  287.5 4.2 collective-permute-done
  291.7 4.3 collective-permute-start.1
  296.1 10.1 %collective-permute-done.1 = f32[128,256]{0,1:T(8,128)S(1)} collective-permute-done((f32[128,256]{0,1:T(8,128)S(1)}, f32[128,256]{0,1:T(8,128)S(1)}, u32[]{:S(2)}, u32[]{:S(2)}) %collective-permute-start.1) | collective-permute-done | bytes 131104 | tf_op jit(solution)/shard_map/ppermute | solution.py:19
  308.1 4.2 collective-permute-done.2
  312.3 5.6 %collective-permute-start.3 = (f32[128,256]{0,1:T(8,128)S(1)}, f32[128,256]{0,1:T(8,128)S(1)}, u32[]{:S(2)}, u32[]{:S(2)}) collective-permute-start(f32[128,256]{0,1:T(8,128)S(1)} %collective-permute-done.2), channel_id=1, source_target_pairs={{0,2},{2,0},{1,3},{3,1},{4,6},{6,4},{5,7},{7,5},{8,10},{10,8},{9,1... | collective-permute-start | bytes 393224 | tf_op jit(solution)/shard_map/ppermute | solution.py:19
  317.9 4.8 %collective-permute-done.3 = f32[128,256]{0,1:T(8,128)S(1)} collective-permute-done((f32[128,256]{0,1:T(8,128)S(1)}, f32[128,256]{0,1:T(8,128)S(1)}, u32[]{:S(2)}, u32[]{:S(2)}) %collective-permute-start.3) | collective-permute-done | bytes 131104 | tf_op jit(solution)/shard_map/ppermute | solution.py:19
  325.6 5.1 %collective-permute-done.4 = f32[128,256]{0,1:T(8,128)S(1)} collective-permute-done((f32[128,256]{0,1:T(8,128)S(1)}, f32[128,256]{0,1:T(8,128)S(1)}, u32[]{:S(2)}, u32[]{:S(2)}) %collective-permute-start.4) | collective-permute-done | bytes 131104 | tf_op jit(solution)/shard_map/ppermute | solution.py:19
  332.6 6.6 %collective-permute-done.5 = f32[128,256]{0,1:T(8,128)S(1)} collective-permute-done((f32[128,256]{0,1:T(8,128)S(1)}, f32[128,256]{0,1:T(8,128)S(1)}, u32[]{:S(2)}, u32[]{:S(2)}) %collective-permute-start.5) | collective-permute-done | bytes 131104 | tf_op jit(solution)/shard_map/ppermute | solution.py:19
  339.2 10.1 %collective-permute-start.6 = (f32[128,256]{0,1:T(8,128)S(1)}, f32[128,256]{0,1:T(8,128)S(1)}, u32[]{:S(2)}, u32[]{:S(2)}) collective-permute-start(f32[128,256]{0,1:T(8,128)S(1)} %broadcast_select_fusion.2), channel_id=1, source_target_pairs={{0,256},{256,0},{16,272},{272,16},{32,288},{288,32},{48,304},{304,... | collective-permute-start | bytes 393224 | tf_op jit(solution)/shard_map/ppermute | solution.py:19
  353.6 6.7 %collective-permute-done.7 = f32[128,256]{0,1:T(8,128)S(1)} collective-permute-done((f32[128,256]{0,1:T(8,128)S(1)}, f32[128,256]{0,1:T(8,128)S(1)}, u32[]{:S(2)}, u32[]{:S(2)}) %collective-permute-start.7) | collective-permute-done | bytes 131104 | tf_op jit(solution)/shard_map/ppermute | solution.py:19
  360.4 8.8 %collective-permute-start.8 = (f32[128,128]{0,1:T(8,128)S(1)}, f32[128,128]{0,1:T(8,128)S(1)}, u32[]{:S(2)}, u32[]{:S(2)}) collective-permute-start(f32[128,128]{0,1:T(8,128)S(1)} %get-tuple-element.10), channel_id=1, source_target_pairs={{0,16},{16,0},{32,48},{48,32},{64,80},{80,64},{96,112},{112,96},{1... | collective-permute-start | bytes 196616 | tf_op jit(solution)/shard_map/ppermute | solution.py:19
  370.8 17.7 %all-gather.17.cloned.1.call-done = bf16[4096,768]{1,0:T(8,128)(2,1)} async-done(((bf16[256,768]{1,0:T(8,128)(2,1)}), bf16[4096,768]{1,0:T(8,128)(2,1)}) %all-gather.17.cloned.1.call-update) | async-done | bytes 6291472 | tf_op jit(solution)/shard_map/all_gather | solution.py:118
  388.4 68.0 %all-gather.15.cloned.1.call-done = bf16[4096,256]{1,0:T(8,128)(2,1)} async-done(((bf16[128,256]{1,0:T(8,128)(2,1)}), bf16[4096,256]{1,0:T(8,128)(2,1)}) %all-gather.15.cloned.1.call-update) | async-done | bytes 2097168 | tf_op jit(solution)/shard_map/all_gather | solution.py:115
  456.4 6.0 %convolution_convert_fusion = bf16[256,768]{1,0:T(8,128)(2,1)} fusion(bf16[4096,256]{1,0:T(8,128)(2,1)} %all-gather.15.cloned.1.call-done, bf16[4096,768]{1,0:T(8,128)(2,1)} %all-gather.17.cloned.1.call-done), kind=kOutput, calls=%fused_computation.13 | convolution fusion | flops 1610809344 | bytes 8781824 | tf_op jit(solution)/shard_map/dot_general | solution.py:116
  (81 shorter events, 38.4 us)
Async XLA Ops:
  7.2 9.5 %copy-start = (f32[8,8]{1,0:T(8,128)S(1)}, f32[8,8]{1,0:T(8,128)}, u32[]{:S(2)}) copy-start(f32[8,8]{1,0:T(8,128)} %param.15) | copy-start | bytes 772
  7.2 24.4 %copy-start.2 = (f32[2048]{0:T(1024)S(1)}, f32[2048]{0:T(1024)}, u32[]{:S(2)}) copy-start(f32[2048]{0:T(1024)} %param.14) | copy-start | bytes 24580
  7.2 25.3 %copy-start.3 = (s32[36,2]{0,1:T(2,128)S(1)}, s32[36,2]{0,1:T(2,128)}, u32[]{:S(2)}) copy-start(s32[36,2]{0,1:T(2,128)} %param.17) | copy-start | bytes 868
  7.2 70.0 %all-gather.9.cloned.1.call-start = ((), (), s32[]{:S(2)}) async-start(), calls=%async_computation.1 | async-start | bytes 1114112 | tf_op jit(solution)/shard_map/all_gather | solution.py:107
  8.8 136.0 %all-gather.7.cloned.1.call-start = ((), (), s32[]{:S(2)}) async-start(), calls=%async_computation | async-start | bytes 2162688 | tf_op jit(solution)/shard_map/all_gather | solution.py:106
  9.6 201.8 %all-gather.13.cloned.1.call-start = ((), (), s32[]{:S(2)}) async-start(), calls=%async_computation.3 | async-start | bytes 1114112 | tf_op jit(solution)/shard_map/all_gather | solution.py:107
  86.6 64.4 %copy-start.1 = (bf16[128,256]{1,0:T(8,128)(2,1)S(1)}, bf16[128,256]{1,0:T(8,128)(2,1)}, u32[]{:S(2)}) copy-start(bf16[128,256]{1,0:T(8,128)(2,1)} %param.12) | copy-start | bytes 196612
  151.9 126.9 %all-gather.11.cloned.1.call-start = ((), (), s32[]{:S(2)}) async-start(), calls=%async_computation.2 | async-start | bytes 2162688 | tf_op jit(solution)/shard_map/all_gather | solution.py:106
  152.4 236.0 %all-gather.17.cloned.1.call-start = ((), (), s32[]{:S(2)}) async-start(), calls=%async_computation.5 | async-start | bytes 6684672 | tf_op jit(solution)/shard_map/all_gather | solution.py:118
  153.0 303.4 %all-gather.15.cloned.1.call-start = ((), (), s32[]{:S(2)}) async-start(), calls=%async_computation.4 | async-start | bytes 2162688 | tf_op jit(solution)/shard_map/all_gather | solution.py:115
  285.0 6.7 %collective-permute-start = (f32[128,256]{0,1:T(8,128)S(1)}, f32[128,256]{0,1:T(8,128)S(1)}, u32[]{:S(2)}, u32[]{:S(2)}) collective-permute-start(f32[128,256]{0,1:T(8,128)S(1)} %copy.37), channel_id=1, source_target_pairs={{0,32},{32,0},{16,48},{48,16},{64,96},{96,64},{80,112},{112,80},{1... | collective-permute-start | bytes 393224 | tf_op jit(solution)/shard_map/ppermute | solution.py:19
  291.7 14.5 %collective-permute-start.1 = (f32[128,256]{0,1:T(8,128)S(1)}, f32[128,256]{0,1:T(8,128)S(1)}, u32[]{:S(2)}, u32[]{:S(2)}) collective-permute-start(f32[128,256]{0,1:T(8,128)S(1)} %collective-permute-done), channel_id=1, source_target_pairs={{0,1},{1,0},{2,3},{3,2},{4,5},{5,4},{6,7},{7,6},{8,9},{9,8},{10,11... | collective-permute-start | bytes 393224 | tf_op jit(solution)/shard_map/ppermute | solution.py:19
  306.2 6.1 %collective-permute-start.2 = (f32[128,256]{0,1:T(8,128)S(1)}, f32[128,256]{0,1:T(8,128)S(1)}, u32[]{:S(2)}, u32[]{:S(2)}) collective-permute-start(f32[128,256]{0,1:T(8,128)S(1)} %broadcast_select_fusion), channel_id=1, source_target_pairs={{0,64},{64,0},{16,80},{80,16},{32,96},{96,32},{48,112},{112,48},{1... | collective-permute-start | bytes 393224 | tf_op jit(solution)/shard_map/ppermute | solution.py:19
  312.3 10.4 %collective-permute-start.3 = (f32[128,256]{0,1:T(8,128)S(1)}, f32[128,256]{0,1:T(8,128)S(1)}, u32[]{:S(2)}, u32[]{:S(2)}) collective-permute-start(f32[128,256]{0,1:T(8,128)S(1)} %collective-permute-done.2), channel_id=1, source_target_pairs={{0,2},{2,0},{1,3},{3,1},{4,6},{6,4},{5,7},{7,5},{8,10},{10,8},{9,1... | collective-permute-start | bytes 393224 | tf_op jit(solution)/shard_map/ppermute | solution.py:19
  322.7 8.0 %collective-permute-start.4 = (f32[128,256]{0,1:T(8,128)S(1)}, f32[128,256]{0,1:T(8,128)S(1)}, u32[]{:S(2)}, u32[]{:S(2)}) collective-permute-start(f32[128,256]{0,1:T(8,128)S(1)} %broadcast_select_fusion.1), channel_id=1, source_target_pairs={{0,128},{128,0},{16,144},{144,16},{32,160},{160,32},{48,176},{176,... | collective-permute-start | bytes 393224 | tf_op jit(solution)/shard_map/ppermute | solution.py:19
  330.7 8.5 %collective-permute-start.5 = (f32[128,256]{0,1:T(8,128)S(1)}, f32[128,256]{0,1:T(8,128)S(1)}, u32[]{:S(2)}, u32[]{:S(2)}) collective-permute-start(f32[128,256]{0,1:T(8,128)S(1)} %collective-permute-done.4), channel_id=1, source_target_pairs={{0,4},{4,0},{1,5},{5,1},{2,6},{6,2},{3,7},{7,3},{8,12},{12,8},{9,1... | collective-permute-start | bytes 393224 | tf_op jit(solution)/shard_map/ppermute | solution.py:19
  339.2 12.4 %collective-permute-start.6 = (f32[128,256]{0,1:T(8,128)S(1)}, f32[128,256]{0,1:T(8,128)S(1)}, u32[]{:S(2)}, u32[]{:S(2)}) collective-permute-start(f32[128,256]{0,1:T(8,128)S(1)} %broadcast_select_fusion.2), channel_id=1, source_target_pairs={{0,256},{256,0},{16,272},{272,16},{32,288},{288,32},{48,304},{304,... | collective-permute-start | bytes 393224 | tf_op jit(solution)/shard_map/ppermute | solution.py:19
  351.6 8.7 %collective-permute-start.7 = (f32[128,256]{0,1:T(8,128)S(1)}, f32[128,256]{0,1:T(8,128)S(1)}, u32[]{:S(2)}, u32[]{:S(2)}) collective-permute-start(f32[128,256]{0,1:T(8,128)S(1)} %collective-permute-done.6), channel_id=1, source_target_pairs={{0,8},{8,0},{1,9},{9,1},{2,10},{10,2},{3,11},{11,3},{4,12},{12,4},... | collective-permute-start | bytes 393224 | tf_op jit(solution)/shard_map/ppermute | solution.py:19
  360.4 9.6 %collective-permute-start.8 = (f32[128,128]{0,1:T(8,128)S(1)}, f32[128,128]{0,1:T(8,128)S(1)}, u32[]{:S(2)}, u32[]{:S(2)}) collective-permute-start(f32[128,128]{0,1:T(8,128)S(1)} %get-tuple-element.10), channel_id=1, source_target_pairs={{0,16},{16,0},{32,48},{48,32},{64,80},{80,64},{96,112},{112,96},{1... | collective-permute-start | bytes 196616 | tf_op jit(solution)/shard_map/ppermute | solution.py:19
Sparse Core Ops, SparseCore 0:
  11.6 65.5 all-gather.8
  79.9 64.8 all-gather.6
  152.0 59.2 all-gather.12
  213.9 64.8 all-gather.10
  281.7 106.6 all-gather.16
  391.0 65.4 all-gather.14
where the time goes:
time: 470 us; the launch traced here: 469 us
  waiting for transfers between devices  351 us (75%)
  starting transfers between devices  40.1 us (9%)
  local copies, waits for them, and re-layouts  29.5 us (6%)
  other arithmetic  24.7 us (5%)
  between operations  14.6 us (3%)
  matrix products  9.24 us (2%)
    all_gather x2, waiting for transfers between devices, body(): column_panel = lax.all_gather(rounded, 'row', axis=0, tiled=True)  116 us
    all_gather x2, waiting for transfers between devices, body(): row_panel = lax.all_gather(rounded, 'col', axis=1, tiled=True)  102 us
    all_gather x1, waiting for transfers between devices, body(): lax.all_gather(sym_amps.astype(jnp.bfloat16), 'row', axis=0, tiled=True)  68 us
    ppermute x9, waiting for transfers between devices, swapped(): return lax.ppermute(block, axis, route)  44.9 us
    ppermute x9, starting transfers between devices, swapped(): return lax.ppermute(block, axis, route)  39.9 us
    all_gather x1, waiting for transfers between devices, body(): lax.all_gather(fitted_ints, 'col', axis=0, tiled=True)  17.7 us
    gather x2, local copies, waits for them, and re-layouts, body(): picked_cols = jnp.take(row_panel, col_position, axis=1).astype(jnp.float32)  12.4 us
    gather x2, local copies, waits for them, and re-layouts, body(): jnp.take(column_panel, row_position, axis=0).astype(jnp.float32)  10.8 us
  transfers between devices with their start and end apart: 15, of which 15 were waited for; matrix products, arithmetic and copies ran while one was open for 10% of the time, Pallas kernels for 0%

commit v1 on v0

v1 whole, which is shorter than its diff:
```python
import jax
import jax.numpy as jnp
from jax import lax
from jax.experimental import pallas as pl
from jax.experimental.pallas import tpu as pltpu
from jax.sharding import PartitionSpec as P

ITERS = 2
MESH = pl.DeviceIdType.MESH
F32 = jnp.float32
BF16 = jnp.bfloat16
ROWS, COLS, DOM, NORB = 128, 256, 512, 8
NY, NX, NZ = 8, 4, 4
FIRST_ROWS = 192
MAX_COPIES = 128


def turn(place, by, count):
    return lax.rem(place + (by + count), count)


def kernel(
    amps, exch, fitted, scal, dom, dom_cols, own_row_dom, own_col_dom, row_level, col_level,
    sym_out, gamma_out,
    fit_all, left_all, right_all, left_part, left_sib, left_zsend, left_zrecv, right_part,
    right_recv, left_hot, right_hot, mir_send, mir_recv, sym_all, acc, send_sems, recv_sems, own_sem,
):
    row = lax.axis_index("row")
    col = lax.axis_index("col")
    y, quarter = row // 4, lax.rem(row, 4)
    zl, core = quarter // 2, lax.rem(quarter, 2)
    x, zh = col // 4, lax.rem(col, 4)
    b2, half = zh // 2, lax.rem(zh, 2)
    orb = col // 2

    def device(y_=y, zl_=zl, core_=core, x_=x, zh_=zh):
        return {"row": y_ * 4 + zl_ * 2 + core_, "col": x_ * 4 + zh_}

    y_up, y_down = device(y_=turn(y, 1, NY)), device(y_=turn(y, -1, NY))
    x_up, x_down = device(x_=turn(x, 1, NX)), device(x_=turn(x, -1, NX))
    z_up, z_down = device(zh_=turn(zh, 1, NZ)), device(zh_=turn(zh, -1, NZ))
    z_far = device(zh_=turn(zh, 2, NZ))
    z_pair = device(zl_=1 - zl)
    sibling = device(core_=1 - core)
    half_pair = device(zh_=b2 * 2 + 1 - half)
    diagonal = row // 2 == col
    mirror = [
        {"row": col * 2 + t, "col": row // 2} for t in range(2)
    ]
    mine = [jnp.logical_and(diagonal, core == t) for t in range(2)]

    barrier = pltpu.get_barrier_semaphore()
    partners = [y_up, y_down, x_up, x_down, z_up, z_down, z_far, z_pair, sibling]
    for partner in partners:
        pl.semaphore_signal(barrier, inc=1, device_id=partner, device_id_type=MESH)
    for t in range(2):

        @pl.when(jnp.logical_not(mine[t]))
        def _():
            pl.semaphore_signal(barrier, inc=1, device_id=mirror[t], device_id_type=MESH)

    pl.semaphore_wait(barrier, len(partners) + 2 - diagonal.astype(jnp.int32))

    sent = []
    sites = [0]

    def send(src, dst, target):
        site = sites[0]
        sites[0] += 1
        copy = pltpu.make_async_remote_copy(
            src_ref=src, dst_ref=dst, send_sem=send_sems.at[site], recv_sem=recv_sems.at[site],
            device_id=target, device_id_type=MESH,
        )
        copy.start()
        sent.append(copy)
        return copy

    def fit_gather(low, count, first_is_z):
        if first_is_z:
            one, two, n = zh, x, NZ
            one_up, one_down, two_up, two_down = z_up, z_down, x_up, x_down
            slot = lambda i, j: j * 4 + i
        else:
            one, two, n = x, zh, NX
            one_up, one_down, two_up, two_down = x_up, x_down, z_up, z_down
            slot = lambda i, j: i * 4 + j

        def at(i, j, piece=None):
            if piece is None:
                return fit_all.at[slot(i, j), pl.ds(low, count), :]
            return fit_all.at[slot(i, j), pl.ds(low + piece * (count // 2), count // 2), :]

        offsets = (0, -1, 1, 2)
        held = {}
        state = {}

        def along_two(d, src=None):
            i = turn(one, d, n)
            src = at(i, two) if src is None else src
            held[d] = (send(src, at(i, two), two_up), send(src, at(i, two), two_down))

        def start():
            own = fitted.at[pl.ds(low, count), :]
            state["up"] = send(own, at(one, two), one_up)
            state["down"] = send(own, at(one, two), one_down)
            along_two(0, own)

        def step_one():
            state["up"].wait_recv()
            i = turn(one, -1, n)
            state["far_up"] = send(at(i, two, 0), at(i, two, 0), one_up)
            along_two(-1)
            state["down"].wait_recv()
            i = turn(one, 1, n)
            state["far_down"] = send(at(i, two, 1), at(i, two, 1), one_down)
            along_two(1)

        def step_two():
            state["far_up"].wait_recv()
            state["far_down"].wait_recv()
            along_two(2)

        far = {}

        def step_three(d):
            up, down = held[d]
            i = turn(one, d, n)
            up.wait_recv()
            j = turn(two, -1, n)
            first = send(at(i, j, 0), at(i, j, 0), two_up)
            down.wait_recv()
            j = turn(two, 1, n)
            far[d] = (first, send(at(i, j, 1), at(i, j, 1), two_down))

        def step_four():
            for d in offsets:
                for copy in far[d]:
                    copy.wait_recv()

        return start, step_one, step_two, step_three, step_four

    fit_a = fit_gather(0, FIRST_ROWS, True)
    fit_b = fit_gather(FIRST_ROWS, COLS - FIRST_ROWS, False)
    own_fit = pltpu.make_async_copy(fitted, fit_all.at[col], own_sem)

    def build_hots():
        for k in range(NORB):
            picked = dom[k : k + 1, pl.ds(pl.multiple_of(quarter * ROWS, ROWS), ROWS)]
            left_hot[k] = jnp.where(own_row_dom[...] == picked, 1.0, 0.0).astype(BF16)
            picked = dom_cols[pl.ds(pl.multiple_of(half * COLS, COLS), COLS), k : k + 1]
            right_hot[k] = jnp.where(picked == own_col_dom[...], 1.0, 0.0).astype(BF16)

    def iteration(t, current, hooks):
        rounded = current.astype(BF16)
        left_all[t, y] = rounded
        right_all[t, orb] = rounded
        lefts, rights = left_all.at[t], right_all.at[t]
        far = send(rights.at[orb], rights.at[orb], z_far)
        up = send(lefts.at[y], lefts.at[y], y_up)
        down = send(lefts.at[y], lefts.at[y], y_down)
        x_one = (
            send(rights.at[orb], rights.at[orb], x_up),
            send(rights.at[orb], rights.at[orb], x_down),
        )
        hooks[0]()
        left_part[t] = jnp.zeros((2, 2, ROWS, COLS), F32)
        right_part[t] = jnp.zeros((2, ROWS, COLS), F32)

        def left_add(k):
            term = jnp.dot(left_hot[k], left_all[t, k], preferred_element_type=F32) * scal[k]
            left_part[t] += term.reshape(2, 2, ROWS, COLS)

        def right_add(k):
            term = jnp.dot(right_all[t, k], right_hot[k], preferred_element_type=F32) * scal[NORB + k]
            right_part[t, 0] += term[:, :COLS]
            right_part[t, 1] += term[:, COLS:]

        other = x * 2 + 1 - b2
        far.wait_recv()
        x_two = (
            send(rights.at[other], rights.at[other], x_up),
            send(rights.at[other], rights.at[other], x_down),
        )

        def y_step(distance, up, down):
            up.wait_recv()
            below = turn(y, -distance, NY)
            down.wait_recv()
            above = turn(y, distance, NY)
            if distance < 3:
                up = send(lefts.at[below], lefts.at[below], y_up)
                down = send(lefts.at[above], lefts.at[above], y_down)
            else:
                low, high = pl.ds(0, ROWS // 2), pl.ds(ROWS // 2, ROWS // 2)
                up = send(lefts.at[below, low], lefts.at[below, low], y_up)
                down = send(lefts.at[above, high], lefts.at[above, high], y_down)
            return below, above, up, down

        def x_step(copies, bit):
            low, high = pl.ds(0, ROWS // 2), pl.ds(ROWS // 2, ROWS // 2)
            copies[0].wait_recv()
            below = turn(x, -1, NX) * 2 + bit
            up = send(rights.at[below, low], rights.at[below, low], x_up)
            copies[1].wait_recv()
            above = turn(x, 1, NX) * 2 + bit
            down = send(rights.at[above, high], rights.at[above, high], x_down)
            return below, above, up, down

        below, above, up, down = y_step(1, up, down)
        x_below, x_above, far_up_one, far_down_one = x_step(x_one, b2)
        right_add(other)
        left_add(below)
        left_add(above)
        below, above, up, down = y_step(2, up, down)
        x_below_two, x_above_two, far_up_two, far_down_two = x_step(x_two, 1 - b2)
        right_add(x_below)
        right_add(x_above)
        left_add(below)
        left_add(above)
        below, above, up, down = y_step(3, up, down)
        right_add(x_below_two)
        right_add(x_above_two)
        left_add(below)
        left_add(above)
        across = turn(x, 2, NX) * 2
        far_up_one.wait_recv()
        far_down_one.wait_recv()
        right_add(across + b2)
        far_up_two.wait_recv()
        far_down_two.wait_recv()
        right_add(across + 1 - b2)
        right_copy = send(right_part.at[t, 1 - half], right_recv.at[t], half_pair)
        up.wait_recv()
        down.wait_recv()
        left_add(turn(y, 4, NY))
        sib_copy = send(left_part.at[t, 1 - core], left_sib.at[t], sibling)
        hooks[1]()
        sib_copy.wait_recv()
        left_zsend[t] = left_part[t, core, 1 - zl] + left_sib[t, 1 - zl]
        z_copy = send(left_zsend.at[t], left_zrecv.at[t], z_pair)
        hooks[2]()
        right_copy.wait_recv()
        right_term = right_part[t, half] + right_recv[t]
        z_copy.wait_recv()
        left_term = left_part[t, core, zl] + left_sib[t, zl] + left_zrecv[t]
        denominator = row_level[...] + col_level[...]
        return scal[2 * NORB] * ((left_term + right_term - exch[...].astype(F32)) / denominator)

    def start_fitted():
        fit_a[0]()
        fit_b[0]()
        own_fit.start()
        build_hots()

    def nothing():
        pass

    def fit_one():
        fit_b[1]()
        fit_a[1]()

    def fit_two():
        fit_b[2]()
        fit_a[2]()

    current = iteration(0, amps[...], (start_fitted, nothing, nothing))
    fit_one()
    current = iteration(1, current, (nothing, nothing, fit_two))

    mir_sites = sites[0]
    sites[0] += 2
    mir_copies = []
    for t in range(2):
        mir_send[t] = current[:, t * ROWS : (t + 1) * ROWS].T
        mir_copies.append(
            pltpu.make_async_remote_copy(
                src_ref=mir_send.at[t], dst_ref=mir_recv.at[core],
                send_sem=send_sems.at[mir_sites + t], recv_sem=recv_sems.at[mir_sites + core],
                device_id=mirror[t], device_id_type=MESH,
            )
        )

        @pl.when(jnp.logical_not(mine[t]))
        def _():
            mir_copies[t].start()

        @pl.when(mine[t])
        def _():
            mir_recv[t] = mir_send[t]

    for t in range(2):

        @pl.when(jnp.logical_not(mine[t]))
        def _():
            pltpu.make_async_remote_copy(
                src_ref=mir_send.at[t], dst_ref=mir_recv.at[t],
                send_sem=send_sems.at[mir_sites + t], recv_sem=recv_sems.at[mir_sites + t],
                device_id=mirror[t], device_id_type=MESH,
            ).wait_recv()

    sym_halves = [
        0.5 * (current[:, t * ROWS : (t + 1) * ROWS] + mir_recv[t]) for t in range(2)
    ]
    for t in range(2):
        sym_out[:, t * ROWS : (t + 1) * ROWS] = sym_halves[t]
        sym_all[y, core, zl, t * ROWS : (t + 1) * ROWS] = sym_halves[t].T.astype(BF16)

    own_block = sym_all.at[y, core, zl]
    pair_block = sym_all.at[y, core, 1 - zl]
    pair_copy = send(own_block, own_block, z_pair)
    up_own = send(own_block, own_block, y_up)
    down_own = send(own_block, own_block, y_down)
    pair_copy.wait_recv()
    up_pair = send(pair_block, pair_block, y_up)
    down_pair = send(pair_block, pair_block, y_down)
    blocks = sym_all.at[y, core]
    sib_copies = [(y, send(blocks, blocks, sibling))]
    up_own.wait_recv()
    up_pair.wait_recv()
    below = sym_all.at[turn(y, -1, NY), core]
    up = send(below, below, y_up)
    sib_copies.append((turn(y, -1, NY), send(below, below, sibling)))
    down_own.wait_recv()
    down_pair.wait_recv()
    above = sym_all.at[turn(y, 1, NY), core]
    down = send(above, above, y_down)
    sib_copies.append((turn(y, 1, NY), send(above, above, sibling)))
    for d in (0, -1, 1, 2):
        fit_b[3](d)
        fit_a[3](d)
    up.wait_recv()
    below = sym_all.at[turn(y, -2, NY), core]
    up = send(below, below, y_up)
    sib_copies.append((turn(y, -2, NY), send(below, below, sibling)))
    down.wait_recv()
    above = sym_all.at[turn(y, 2, NY), core]
    down = send(above, above, y_down)
    sib_copies.append((turn(y, 2, NY), send(above, above, sibling)))
    up.wait_recv()
    low = sym_all.at[turn(y, -3, NY), core, 0]
    far_up = send(low, low, y_up)
    below = sym_all.at[turn(y, -3, NY), core]
    sib_copies.append((turn(y, -3, NY), send(below, below, sibling)))
    down.wait_recv()
    high = sym_all.at[turn(y, 3, NY), core, 1]
    far_down = send(high, high, y_down)
    above = sym_all.at[turn(y, 3, NY), core]
    sib_copies.append((turn(y, 3, NY), send(above, above, sibling)))
    far_up.wait_recv()
    far_down.wait_recv()
    across = sym_all.at[turn(y, 4, NY), core]
    sib_copies.append((turn(y, 4, NY), send(across, across, sibling)))

    own_fit.wait()
    fit_b[4]()
    fit_a[4]()
    acc[...] = jnp.zeros(acc.shape, F32)
    for k, copy in sib_copies:
        copy.wait_recv()
        panel = jnp.concatenate(
            [sym_all[k, 0, 0], sym_all[k, 1, 0], sym_all[k, 0, 1], sym_all[k, 1, 1]], axis=1
        )
        right = jnp.concatenate([fit_all[k * 2], fit_all[k * 2 + 1]], axis=0)
        acc[...] += jnp.dot(panel, right, preferred_element_type=F32)
    gamma_out[...] = acc[...].astype(BF16)

    for copy in sent:
        copy.wait_send()
    for t in range(2):

        @pl.when(jnp.logical_not(mine[t]))
        def _():
            mir_copies[t].wait_send()


def lookup(values_table, indices):
    extent = values_table.shape[0]
    matches = indices[:, None] == jnp.arange(extent, dtype=jnp.int32)[None, :]
    return jnp.sum(jnp.where(matches, values_table[None, :], 0.0), axis=1)


def body(start_amps, exchange_ints, fitted_ints, pao_energy, occ_fock, domains, pair_list):
    row = lax.axis_index("row")
    col = lax.axis_index("col")
    first, second = row // 4, col // 2
    orbits = jnp.arange(NORB, dtype=jnp.int32)
    first_fock = lax.dynamic_index_in_dim(occ_fock, first, 0, keepdims=False)
    second_fock = lax.dynamic_index_in_dim(occ_fock, second, 0, keepdims=False)
    first_own = jnp.sum(jnp.where(orbits == first, first_fock, 0.0))
    second_own = jnp.sum(jnp.where(orbits == second, second_fock, 0.0))
    first_off = jnp.where(orbits == first, 0.0, first_fock)
    second_off = jnp.where(orbits == second, 0.0, second_fock)
    listed = jnp.any((pair_list[:, 0] == first) & (pair_list[:, 1] == second)).astype(F32)
    scal = jnp.concatenate([first_off, second_off, jnp.broadcast_to(listed, (NORB,))])
    first_dom = lax.dynamic_index_in_dim(domains, first, 0, keepdims=False)
    second_dom = lax.dynamic_index_in_dim(domains, second, 0, keepdims=False)
    own_row_dom = first_dom.reshape(2, 2, ROWS).transpose(1, 0, 2).reshape(DOM, 1)
    own_col_dom = second_dom.reshape(1, DOM)
    row_paos = lax.dynamic_slice_in_dim(first_dom, lax.rem(row, 4) * ROWS, ROWS)
    col_paos = lax.dynamic_slice_in_dim(second_dom, lax.rem(col, 2) * COLS, COLS)
    row_level = (lookup(pao_energy, row_paos) - first_own)[:, None]
    col_level = (lookup(pao_energy, col_paos) - second_own)[None, :]
    vmem = pl.BlockSpec(memory_space=pltpu.VMEM)
    smem = pl.BlockSpec(memory_space=pltpu.SMEM)
    hbm = pl.BlockSpec(memory_space=pl.ANY)
    width = fitted_ints.shape[1]
    return pl.pallas_call(
        kernel,
        out_shape=(
            jax.ShapeDtypeStruct((ROWS, COLS), F32),
            jax.ShapeDtypeStruct((COLS, width), BF16),
        ),
        in_specs=[vmem, vmem, hbm, smem, vmem, vmem, vmem, vmem, vmem, vmem],
        out_specs=(vmem, vmem),
        scratch_shapes=[
            pltpu.VMEM((NX * NZ, COLS, width), BF16),
            pltpu.VMEM((ITERS, NORB, ROWS, COLS), BF16),
            pltpu.VMEM((ITERS, NORB, ROWS, COLS), BF16),
            pltpu.VMEM((ITERS, 2, 2, ROWS, COLS), F32),
            pltpu.VMEM((ITERS, 2, ROWS, COLS), F32),
            pltpu.VMEM((ITERS, ROWS, COLS), F32),
            pltpu.VMEM((ITERS, ROWS, COLS), F32),
            pltpu.VMEM((ITERS, 2, ROWS, COLS), F32),
            pltpu.VMEM((ITERS, ROWS, COLS), F32),
            pltpu.VMEM((NORB, DOM, ROWS), BF16),
            pltpu.VMEM((NORB, COLS, DOM), BF16),
            pltpu.VMEM((2, ROWS, ROWS), F32),
            pltpu.VMEM((2, ROWS, ROWS), F32),
            pltpu.VMEM((NY, 2, 2, COLS, ROWS), BF16),
            pltpu.VMEM((COLS, width), F32),
            pltpu.SemaphoreType.DMA((MAX_COPIES,)),
            pltpu.SemaphoreType.DMA((MAX_COPIES,)),
            pltpu.SemaphoreType.DMA,
        ],
        compiler_params=pltpu.CompilerParams(
            collective_id=0, has_side_effects=True, vmem_limit_bytes=48 * 1024 * 1024
        ),
        cost_estimate=pl.CostEstimate(flops=2_000_000_000, bytes_accessed=20_000_000, transcendentals=0),
    )(
        start_amps, exchange_ints, fitted_ints, scal, domains, domains.T, own_row_dom, own_col_dom,
        row_level, col_level,
    )


def solution(mesh):
    return jax.shard_map(
        body,
        mesh=mesh,
        in_specs=(P("row", "col"), P("row", "col"), P("col", "row"), P(), P(), P(), P()),
        out_specs=(P("row", "col"), P("col", "row")),
        check_vma=False,
    )
```

time: 470 us -> 147 us (0.31)
  waiting for transfers between devices: 351 us -> 0 us
  Pallas kernels: 0 us -> 133 us
  starting transfers between devices: 40.1 us -> 0 us
  local copies, waits for them, and re-layouts: 29.5 us -> 4.24 us
  other arithmetic: 24.7 us -> 6.17 us
  between operations: 14.6 us -> 1.45 us
  matrix products: 9.24 us -> 0 us
    all_gather x6 -> x0, waiting for transfers between devices: 304 us -> none  [the longest x2 116 us: body(): column_panel = lax.all_gather(rounded, 'row', axis=0, tiled=True)]
    pallas_call x0 -> x1, Pallas kernels: none -> 133 us  [body(): pl.pallas_call(kernel, out_shape=(jax.ShapeDtypeStruct((ROWS, COLS), F32)...]
    ppermute x9 -> x0, waiting for transfers between devices: 44.9 us -> none  [swapped(): return lax.ppermute(block, axis, route)]
    ppermute x9 -> x0, starting transfers between devices: 39.9 us -> none  [swapped(): return lax.ppermute(block, axis, route)]
    gather x5 -> x0, local copies, waits for them, and re-layouts: 23.8 us -> none  [the longest x2 12.4 us: body(): picked_cols = jnp.take(row_panel, col_position, axis=1).astype(jnp.float32)]
    dot_general x10 -> x0, matrix products: 9.24 us -> none  [the longest x1 5.99 us: body(): lax.dot_general(sym_panel, lax.all_gather(fitted_ints, 'col', axis=0, til...]
    reduce_sum x2 -> x1, other arithmetic: 9.28 us -> 1.38 us  [body(): second_own = jnp.sum(jnp.where(orbits == second, second_fock, 0.0))]
    reduce_or x2 -> x1, other arithmetic: 9.29 us -> 1.4 us  [body(): jnp.any((pair_list[:, 0] == first) & (pair_list[:, 1] == second))]
  transfers between devices with their start and end apart: 15 -> 0, of which waited for: 15 -> 0; matrix products, arithmetic and copies ran while one was open for 10% -> 0% of each run, Pallas kernels for 0% -> 0%
where the time goes in v1:
time: 147 us; the launch traced here: 145 us
  Pallas kernels  133 us (90%)
  other arithmetic  6.17 us (4%)
  local copies, waits for them, and re-layouts  4.24 us (3%)
    pallas_call x1, Pallas kernels, body(): pl.pallas_call(kernel, out_shape=(jax.ShapeDtypeStruct((ROWS, COLS), F32)...  133 us

profile of v1, /device:TPU:1, one launch (start us, length us, event | category | flops | bytes accessed | tf_op | source)
XLA Modules:
  0.0 145.2 jit_solution(17114477190456390612)
XLA Ops:
  0.6 0.0 copy-start
  0.6 0.0 copy-start.1
  0.7 0.0 copy-start.2
  0.7 0.0 copy-start.3
  0.7 0.8 dynamic-slice_bitcast_fusion
  1.6 0.9 select_reduce_fusion.1
  2.5 0.8 dynamic_slice.25
  3.3 1.1 select_reduce_fusion
  4.4 1.4 and_reduce_fusion
  6.4 1.4 fusion.3
  7.8 0.6 broadcast_subtract_fusion
  8.5 0.7 subtract_bitcast_fusion
  9.1 0.1 pad_maximum_fusion.scal
  9.2 0.8 constant_dynamic-slice_fusion
  10.0 0.1 copy.18.row_level
  10.1 0.1 copy.17.own_row_dom
  10.3 0.0 copy-done
  10.3 0.1 copy.15
  10.4 0.0 copy-done.1
  10.4 0.0 copy-done.2
  10.4 0.0 copy-done.3
  10.5 133.4 %shard_map.86 = (f32[128,256]{1,0:T(8,128)S(1)}, bf16[256,768]{1,0:T(8,128)(2,1)S(1)}) custom-call(f32[128,256]{1,0:T(8,128)S(1)} %copy-done.2, bf16[128,256]{1,0:T(8,128)(2,1)S(1)} %copy-done.3, bf16[256,768]{1,0:T(8,128)(2,1)S(1)} %copy-done.1, f32[24]{0:T(128)S(1)} %pad_maximum_fusion.scal, s32[8,512]{1,0:T(8,128)S(1)} %copy-done, s32[512,8]{1,0:T(8,128)S(1)} %bitcast.23, ...), custom_call_target="tpu_custom_call" | custom-call | flops 2000000000 | bytes 20000000 | tf_op jit(solution)/shard_map/pallas_call | solution.py:407
  143.8 0.7 copy.21
  144.5 0.7 copy.22
  (2 shorter events, 0.0 us)
Async XLA Ops:
  0.6 9.7 %copy-start = (s32[8,512]{1,0:T(8,128)S(1)}, s32[8,512]{1,0:T(8,128)}, u32[]{:S(2)}) copy-start(s32[8,512]{1,0:T(8,128)} %dom.1) | copy-start | bytes 49156
  0.6 9.8 %copy-start.1 = (bf16[256,768]{1,0:T(8,128)(2,1)S(1)}, bf16[256,768]{1,0:T(8,128)(2,1)}, u32[]{:S(2)}) copy-start(bf16[256,768]{1,0:T(8,128)(2,1)} %fitted.1) | copy-start | bytes 1179652
  0.7 9.8 %copy-start.2 = (f32[128,256]{1,0:T(8,128)S(1)}, f32[128,256]{1,0:T(8,128)}, u32[]{:S(2)}) copy-start(f32[128,256]{1,0:T(8,128)} %amps.1) | copy-start | bytes 393220
  0.7 9.8 %copy-start.3 = (bf16[128,256]{1,0:T(8,128)(2,1)S(1)}, bf16[128,256]{1,0:T(8,128)(2,1)}, u32[]{:S(2)}) copy-start(bf16[128,256]{1,0:T(8,128)(2,1)} %exch.1) | copy-start | bytes 196612

commit v2 on v1

v2 whole, which is shorter than its diff:
```python
import jax
import jax.numpy as jnp
from jax import lax
from jax.experimental import pallas as pl
from jax.experimental.pallas import tpu as pltpu
from jax.sharding import PartitionSpec as P

ITERS = 2
MESH = pl.DeviceIdType.MESH
F32 = jnp.float32
BF16 = jnp.bfloat16
ROWS, COLS, DOM, NORB = 128, 256, 512, 8
NY, NX, NZ = 8, 4, 4
FIRST_ROWS = 192
MAX_COPIES = 128


def turn(place, by, count):
    return lax.rem(place + (by + count), count)


def kernel(
    amps, exch, fitted, energy, fock, dom, pairs,
    sym_out, gamma_out,
    fit_all, left_all, right_all, left_part, left_sib, right_part, right_recv,
    left_hot, right_hot, levels, mir_send, mir_recv, sym_all, acc, send_sems, recv_sems, own_sem,
):
    row = lax.axis_index("row")
    col = lax.axis_index("col")
    y, quarter = row // 4, lax.rem(row, 4)
    zl, core = quarter // 2, lax.rem(quarter, 2)
    x, zh = col // 4, lax.rem(col, 4)
    b2, half = zh // 2, lax.rem(zh, 2)
    orb = col // 2

    def device(y_=y, zl_=zl, core_=core, x_=x, zh_=zh):
        return {"row": y_ * 4 + zl_ * 2 + core_, "col": x_ * 4 + zh_}

    y_up, y_down = device(y_=turn(y, 1, NY)), device(y_=turn(y, -1, NY))
    x_far = device(x_=turn(x, 2, NX))
    x_up, x_down = device(x_=turn(x, 1, NX)), device(x_=turn(x, -1, NX))
    z_up, z_down = device(zh_=turn(zh, 1, NZ)), device(zh_=turn(zh, -1, NZ))
    z_far = device(zh_=turn(zh, 2, NZ))
    z_pair = device(zl_=1 - zl)
    sibling = device(core_=1 - core)
    half_pair = device(zh_=b2 * 2 + 1 - half)
    diagonal = row // 2 == col
    mirror = [
        {"row": col * 2 + t, "col": row // 2} for t in range(2)
    ]
    mine = [jnp.logical_and(diagonal, core == t) for t in range(2)]

    barrier = pltpu.get_barrier_semaphore()
    partners = [y_up, y_down, x_up, x_down, x_far, z_up, z_down, z_far, z_pair, sibling]
    for partner in partners:
        pl.semaphore_signal(barrier, inc=1, device_id=partner, device_id_type=MESH)
    for t in range(2):

        @pl.when(jnp.logical_not(mine[t]))
        def _():
            pl.semaphore_signal(barrier, inc=1, device_id=mirror[t], device_id_type=MESH)

    pl.semaphore_wait(barrier, len(partners) + 2 - diagonal.astype(jnp.int32))

    sent = []
    sites = [0]

    def send(src, dst, target):
        site = sites[0]
        sites[0] += 1
        copy = pltpu.make_async_remote_copy(
            src_ref=src, dst_ref=dst, send_sem=send_sems.at[site], recv_sem=recv_sems.at[site],
            device_id=target, device_id_type=MESH,
        )
        copy.start()
        sent.append(copy)
        return copy

    def fit_gather(low, count, first_is_z):
        if first_is_z:
            one, two, n = zh, x, NZ
            one_up, one_down, two_up, two_down = z_up, z_down, x_up, x_down
            slot = lambda i, j: j * 4 + i
        else:
            one, two, n = x, zh, NX
            one_up, one_down, two_up, two_down = x_up, x_down, z_up, z_down
            slot = lambda i, j: i * 4 + j

        def at(i, j, piece=None):
            if piece is None:
                return fit_all.at[slot(i, j), pl.ds(low, count), :]
            return fit_all.at[slot(i, j), pl.ds(low + piece * (count // 2), count // 2), :]

        offsets = (0, -1, 1, 2)
        held = {}
        state = {}

        def along_two(d, src=None):
            i = turn(one, d, n)
            src = at(i, two) if src is None else src
            held[d] = (send(src, at(i, two), two_up), send(src, at(i, two), two_down))

        def start():
            own = fitted.at[pl.ds(low, count), :]
            state["up"] = send(own, at(one, two), one_up)
            state["down"] = send(own, at(one, two), one_down)
            along_two(0, own)

        def step_one():
            state["up"].wait_recv()
            i = turn(one, -1, n)
            state["far_up"] = send(at(i, two, 0), at(i, two, 0), one_up)
            along_two(-1)
            state["down"].wait_recv()
            i = turn(one, 1, n)
            state["far_down"] = send(at(i, two, 1), at(i, two, 1), one_down)
            along_two(1)

        def step_two():
            state["far_up"].wait_recv()
            state["far_down"].wait_recv()
            along_two(2)

        far = {}

        def step_three(d):
            up, down = held[d]
            i = turn(one, d, n)
            up.wait_recv()
            j = turn(two, -1, n)
            first = send(at(i, j, 0), at(i, j, 0), two_up)
            down.wait_recv()
            j = turn(two, 1, n)
            far[d] = (first, send(at(i, j, 1), at(i, j, 1), two_down))

        def step_four():
            for d in offsets:
                for copy in far[d]:
                    copy.wait_recv()

        return start, step_one, step_two, step_three, step_four

    fit_a = fit_gather(0, FIRST_ROWS, True)
    fit_b = fit_gather(FIRST_ROWS, COLS - FIRST_ROWS, False)
    own_fit = pltpu.make_async_copy(fitted, fit_all.at[col], own_sem)

    def listed():
        found = jnp.zeros((), jnp.bool_)
        for p in range(pairs.shape[1]):
            found = found | ((pairs[0, p] == y) & (pairs[1, p] == orb))
        return jnp.where(found, 1.0, 0.0)

    def off_diagonal(own, k):
        return jnp.where(own == k, 0.0, fock[own, k])

    def prepare():
        domains = dom[...].astype(F32)
        columns = jnp.concatenate([domains, jnp.zeros((ROWS - NORB, DOM), F32)], axis=0).T
        lanes = lax.broadcasted_iota(jnp.int32, (DOM, ROWS), 1)

        def column_of(k):
            return jnp.sum(jnp.where(lanes == k, columns, 0.0), axis=1, keepdims=True)

        levels[2] = column_of(y)
        levels[3] = column_of(orb)
        own_rows = levels[2, pl.ds(pl.multiple_of(zl * 2 * ROWS, 2 * ROWS), 2 * ROWS), :]
        own_cols = dom[pl.ds(orb, 1), :].astype(F32)
        for k in range(NORB):
            picked = [
                dom[k : k + 1, pl.ds(pl.multiple_of((p * 2 + core) * ROWS, ROWS), ROWS)] for p in range(2)
            ]
            picked = jnp.concatenate(picked, axis=1).astype(F32)
            left_hot[k] = jnp.where(own_rows == picked, 1.0, 0.0).astype(BF16)
            levels[4] = columns[:, k : k + 1]
            picked = levels[4, pl.ds(pl.multiple_of(half * COLS, COLS), COLS), :]
            right_hot[k] = jnp.where(picked == own_cols, 1.0, 0.0).astype(BF16)

        def level_of(paos):
            found = jnp.zeros((paos.shape[0], ROWS), F32)
            lane = lax.broadcasted_iota(jnp.int32, found.shape, 1).astype(F32)
            for r in range(energy.shape[0]):
                found += jnp.where(paos == lane + r * ROWS, energy[r : r + 1, :], 0.0)
            return jnp.sum(found, axis=1, keepdims=True)

        row_paos = levels[2, pl.ds(pl.multiple_of(quarter * ROWS, ROWS), ROWS), :]
        col_paos = levels[3, pl.ds(pl.multiple_of(half * COLS, COLS), COLS), :]
        row_level = level_of(row_paos) - fock[y, y]
        col_level = level_of(col_paos) - fock[orb, orb]
        return jnp.broadcast_to(row_level, (ROWS, COLS)) + jnp.broadcast_to(col_level, (COLS, ROWS)).T

    def panel_gather(at, between, arrived):
        ends = [lambda: None] * 8 if between is None else between
        pair = send(at(y, zl), at(y, zl), z_pair)
        ups = [send(at(y, zl), at(y, zl), y_up)]
        downs = [send(at(y, zl), at(y, zl), y_down)]
        ends[0]()
        pair.wait_recv()
        ups.append(send(at(y, 1 - zl), at(y, 1 - zl), y_up))
        downs.append(send(at(y, 1 - zl), at(y, 1 - zl), y_down))
        arrived(y, None)
        for distance in (1, 2, 3):
            below, above = turn(y, -distance, NY), turn(y, distance, NY)
            for p, place in enumerate((zl, 1 - zl)):
                ups[p].wait_recv()
                if distance < 3 or p == 0:
                    ups[p] = send(at(below, place), at(below, place), y_up)
                downs[p].wait_recv()
                if distance < 3 or p == 1:
                    downs[p] = send(at(above, place), at(above, place), y_down)
                ends[distance * 2 - 1 + p]()
            arrived(below, distance)
            arrived(above, distance)
        ups[0].wait_recv()
        downs[1].wait_recv()
        arrived(turn(y, 4, NY), 4)
        ends[7]()

    def iteration(t, current, first):
        rounded = current.astype(BF16)
        left_all[t, y, zl] = rounded
        right_all[t, orb] = rounded
        lefts, rights = left_all.at[t], right_all.at[t]
        other = x * 2 + 1 - b2
        far = send(rights.at[orb], rights.at[orb], z_far)
        x_one = [send(rights.at[orb], rights.at[orb], to) for to in (x_up, x_down, x_far)]
        x_two = []
        left_part[t] = jnp.zeros((2, ROWS, COLS), F32)
        right_part[t] = jnp.zeros((2, ROWS, COLS), F32)

        def left_add(k, distance):
            if distance is not None:
                block = left_all[t, k].reshape(2 * ROWS, COLS)
                term = jnp.dot(left_hot[k], block, preferred_element_type=F32) * off_diagonal(y, k)
                left_part[t] += term.reshape(2, ROWS, COLS)

        def right_add(k):
            term = jnp.dot(right_all[t, k], right_hot[k], preferred_element_type=F32)
            term = term * off_diagonal(orb, k)
            right_part[t, 0] += term[:, :COLS]
            right_part[t, 1] += term[:, COLS:]

        def right_far():
            far.wait_recv()
            x_two.extend(send(rights.at[other], rights.at[other], to) for to in (x_up, x_down, x_far))

        def right_one():
            right_add(other)
            for copy, by in zip(x_one, (-1, 1, 2)):
                copy.wait_recv()
                right_add(turn(x, by, NX) * 2 + b2)

        right_copy = []

        def right_two():
            for copy, by in zip(x_two, (-1, 1, 2)):
                copy.wait_recv()
                right_add(turn(x, by, NX) * 2 + 1 - b2)
            right_copy.append(send(right_part.at[t, 1 - half], right_recv.at[t], half_pair))

        def nothing():
            pass

        panel_gather(
            lambda k, p: lefts.at[k, p],
            (first, nothing, right_far, nothing, right_one, nothing, right_two, nothing),
            left_add,
        )
        sib_copy = send(left_part.at[t, 1 - core], left_sib.at[t], sibling)
        right_copy[0].wait_recv()
        right_term = right_part[t, half] + right_recv[t]
        sib_copy.wait_recv()
        left_term = left_part[t, core] + left_sib[t]
        return weight * ((left_term + right_term - exch[...].astype(F32)) / acc[:ROWS, :COLS])

    def start_fitted():
        fit_a[0]()
        fit_b[0]()
        own_fit.start()
        acc[:ROWS, :COLS] = prepare()

    def fit_one():
        fit_b[1]()
        fit_a[1]()

    def fit_two():
        fit_b[2]()
        fit_a[2]()

    weight = listed()
    current = iteration(0, amps[...], start_fitted)
    fit_one()
    current = iteration(1, current, lambda: None)
    fit_two()

    mir_sites = sites[0]
    sites[0] += 2
    mir_copies = []
    for t in range(2):
        mir_send[t] = current[:, t * ROWS : (t + 1) * ROWS].T
        mir_copies.append(
            pltpu.make_async_remote_copy(
                src_ref=mir_send.at[t], dst_ref=mir_recv.at[core],
                send_sem=send_sems.at[mir_sites + t], recv_sem=recv_sems.at[mir_sites + core],
                device_id=mirror[t], device_id_type=MESH,
            )
        )

        @pl.when(jnp.logical_not(mine[t]))
        def _():
            mir_copies[t].start()

        @pl.when(mine[t])
        def _():
            mir_recv[t] = mir_send[t]

    for t in range(2):

        @pl.when(jnp.logical_not(mine[t]))
        def _():
            pltpu.make_async_remote_copy(
                src_ref=mir_send.at[t], dst_ref=mir_recv.at[t],
                send_sem=send_sems.at[mir_sites + t], recv_sem=recv_sems.at[mir_sites + t],
                device_id=mirror[t], device_id_type=MESH,
            ).wait_recv()

    sym_halves = [
        0.5 * (current[:, t * ROWS : (t + 1) * ROWS] + mir_recv[t]) for t in range(2)
    ]
    for t in range(2):
        sym_out[:, t * ROWS : (t + 1) * ROWS] = sym_halves[t]
        sym_all[y, core, zl, t * ROWS : (t + 1) * ROWS] = sym_halves[t].T.astype(BF16)

    sib_copies = []

    def forward(k, distance):
        blocks = sym_all.at[k, core]
        sib_copies.append((k, send(blocks, blocks, sibling)))

    def fit_three(*offsets):
        def run():
            for d in offsets:
                fit_b[3](d)
                fit_a[3](d)

        return run

    def nothing():
        pass

    panel_gather(
        lambda k, p: sym_all.at[k, core, p],
        (nothing, nothing, fit_three(0), nothing, fit_three(-1), nothing, fit_three(1), fit_three(2)),
        forward,
    )
    own_fit.wait()
    fit_b[4]()
    fit_a[4]()
    acc[...] = jnp.zeros(acc.shape, F32)
    for k, copy in sib_copies:
        copy.wait_recv()
        panel = jnp.concatenate(
            [sym_all[k, 0, 0], sym_all[k, 1, 0], sym_all[k, 0, 1], sym_all[k, 1, 1]], axis=1
        )
        right = jnp.concatenate([fit_all[k * 2], fit_all[k * 2 + 1]], axis=0)
        acc[...] += jnp.dot(panel, right, preferred_element_type=F32)
    gamma_out[...] = acc[...].astype(BF16)

    for copy in sent:
        copy.wait_send()
    for t in range(2):

        @pl.when(jnp.logical_not(mine[t]))
        def _():
            mir_copies[t].wait_send()


def body(start_amps, exchange_ints, fitted_ints, pao_energy, occ_fock, domains, pair_list):
    vmem = pl.BlockSpec(memory_space=pltpu.VMEM)
    smem = pl.BlockSpec(memory_space=pltpu.SMEM)
    hbm = pl.BlockSpec(memory_space=pl.ANY)
    width = fitted_ints.shape[1]
    return pl.pallas_call(
        kernel,
        out_shape=(
            jax.ShapeDtypeStruct((ROWS, COLS), F32),
            jax.ShapeDtypeStruct((COLS, width), BF16),
        ),
        in_specs=[vmem, vmem, hbm, vmem, smem, vmem, smem],
        out_specs=(vmem, vmem),
        scratch_shapes=[
            pltpu.VMEM((NX * NZ, COLS, width), BF16),
            pltpu.VMEM((ITERS, NORB, 2, ROWS, COLS), BF16),
            pltpu.VMEM((ITERS, NORB, ROWS, COLS), BF16),
            pltpu.VMEM((ITERS, 2, ROWS, COLS), F32),
            pltpu.VMEM((ITERS, ROWS, COLS), F32),
            pltpu.VMEM((ITERS, 2, ROWS, COLS), F32),
            pltpu.VMEM((ITERS, ROWS, COLS), F32),
            pltpu.VMEM((NORB, 2 * ROWS, 2 * ROWS), BF16),
            pltpu.VMEM((NORB, COLS, DOM), BF16),
            pltpu.VMEM((5, DOM, 1), F32),
            pltpu.VMEM((2, ROWS, ROWS), F32),
            pltpu.VMEM((2, ROWS, ROWS), F32),
            pltpu.VMEM((NY, 2, 2, COLS, ROWS), BF16),
            pltpu.VMEM((COLS, width), F32),
            pltpu.SemaphoreType.DMA((MAX_COPIES,)),
            pltpu.SemaphoreType.DMA((MAX_COPIES,)),
            pltpu.SemaphoreType.DMA,
        ],
        compiler_params=pltpu.CompilerParams(
            collective_id=0, has_side_effects=True, vmem_limit_bytes=48 * 1024 * 1024
        ),
        cost_estimate=pl.CostEstimate(flops=2_000_000_000, bytes_accessed=20_000_000, transcendentals=0),
    )(
        start_amps, exchange_ints, fitted_ints, pao_energy.reshape(-1, ROWS), occ_fock, domains, pair_list.T
    )


def solution(mesh):
    return jax.shard_map(
        body,
        mesh=mesh,
        in_specs=(P("row", "col"), P("row", "col"), P("col", "row"), P(), P(), P(), P()),
        out_specs=(P("row", "col"), P("col", "row")),
        check_vma=False,
    )
```

time: 147 us -> 151 us (1.027)
  Pallas kernels: 133 us -> 142 us
  other arithmetic: 6.17 us -> 0 us
  local copies, waits for them, and re-layouts: 4.24 us -> 6.91 us
    pallas_call x1, Pallas kernels: 133 us -> 142 us  [body(): pl.pallas_call(kernel, out_shape=(jax.ShapeDtypeStruct((ROWS, COLS), F32)...]
    unnamed x11 -> x16, local copies, waits for them, and re-layouts: 1.54 us -> 6.91 us
    reduce_sum x3 -> x0, other arithmetic: 3.4 us -> none  [the longest x2 2.02 us: lookup(): return jnp.sum(jnp.where(matches, values_table[None, :], 0.0), axis=1)]
    dynamic_slice x2 -> x0, local copies, waits for them, and re-layouts: 1.59 us -> none  [the longest x1 0.8 us: body(): second_dom = lax.dynamic_index_in_dim(domains, second, 0, keepdims=False)]
where the time goes in v2:
time: 151 us; the launch traced here: 149 us
  Pallas kernels  142 us (94%)
  local copies, waits for them, and re-layouts  6.91 us (5%)
    pallas_call x1, Pallas kernels, body(): pl.pallas_call(kernel, out_shape=(jax.ShapeDtypeStruct((ROWS, COLS), F32)...  142 us
    unnamed x16, local copies, waits for them, and re-layouts  6.91 us

profile of v2, /device:TPU:1, one launch (start us, length us, event | category | flops | bytes accessed | tf_op | source)
XLA Modules:
  0.0 149.2 jit_solution(12934380319841042758)
XLA Ops:
  0.6 0.0 copy-start.6
  0.6 0.7 copy-done.6
  1.3 0.0 copy-start
  1.3 1.0 copy-done
  2.3 0.0 copy-start.1
  2.3 0.9 copy-done.1
  3.2 0.0 copy-start.2
  3.2 0.8 copy-done.2
  4.1 0.0 copy-start.3
  4.1 0.7 copy-done.3
  4.8 0.0 copy-start.4
  4.8 0.7 copy-done.4
  5.5 0.0 copy-start.5
  5.5 0.7 copy-done.5
  6.2 141.6 %shard_map.86 = (f32[128,256]{1,0:T(8,128)S(1)}, bf16[256,768]{1,0:T(8,128)(2,1)S(1)}) custom-call(f32[128,256]{1,0:T(8,128)S(1)} %copy-done.1, bf16[128,256]{1,0:T(8,128)(2,1)S(1)} %copy-done.2, bf16[256,768]{1,0:T(8,128)(2,1)S(1)} %copy-done, f32[16,128]{1,0:T(8,128)S(1)} %bitcast.2, f32[8,8]{1,0:T(8,128)S(1)} %copy-done.5, s32[8,512]{1,0:T(8,128)S(1)} %copy-done.3, ...), custom_call_target="tpu_custom_call" | custom-call | flops 2000000000 | bytes 20000000 | tf_op jit(solution)/shard_map/pallas_call | solution.py:382
  147.8 0.7 copy.11
  148.5 0.7 copy.12
Async XLA Ops:
  0.6 0.7 copy-start.6
  1.3 1.0 copy-start
  2.3 0.9 copy-start.1
  3.2 0.8 copy-start.2
  4.1 0.7 copy-start.3
  4.8 0.7 copy-start.4
  5.5 0.7 copy-start.5

commit v3 on v2

--- a/solution.py
+++ b/solution.py
@@ -11,8 +11,9 @@
 BF16 = jnp.bfloat16
 ROWS, COLS, DOM, NORB = 128, 256, 512, 8
 NY, NX, NZ = 8, 4, 4
-FIRST_ROWS = 192
-MAX_COPIES = 128
+PIECES = ((0, 256, True),)
+PLAN = {'start': [0], (0, 6): [1, 2], (0, 8): [4], (1, 2): [3], (1, 4): [5], (1, 8): [6], (2, 0): [7], (3, 4): [8, 9, 10, 11]}
+MAX_COPIES = 256
 
 
 def turn(place, by, count):
@@ -20,10 +21,11 @@
 
 
 def kernel(
-    amps, exch, fitted, energy, fock, dom, pairs,
+    amps_hbm, exch_hbm, fitted, energy_hbm, fock, dom_hbm, pairs,
     sym_out, gamma_out,
     fit_all, left_all, right_all, left_part, left_sib, right_part, right_recv,
-    left_hot, right_hot, levels, mir_send, mir_recv, sym_all, acc, send_sems, recv_sems, own_sem,
+    left_hot, right_hot, levels, mir_send, mir_recv, sym_all, acc, amps, exch, energy, dom,
+    send_sems, recv_sems, own_sem, load_sems,
 ):
     row = lax.axis_index("row")
     col = lax.axis_index("col")
@@ -50,6 +52,14 @@
     ]
     mine = [jnp.logical_and(diagonal, core == t) for t in range(2)]
 
+    loads = [
+        pltpu.make_async_copy(src, dst, load_sems.at[n])
+        for n, (src, dst) in enumerate(
+            ((amps_hbm, amps), (dom_hbm, dom), (energy_hbm, energy), (exch_hbm, exch))
+        )
+    ]
+    for load in loads:
+        load.start()
     barrier = pltpu.get_barrier_semaphore()
     partners = [y_up, y_down, x_up, x_down, x_far, z_up, z_down, z_far, z_pair, sibling]
     for partner in partners:
@@ -91,9 +101,9 @@
                 return fit_all.at[slot(i, j), pl.ds(low, count), :]
             return fit_all.at[slot(i, j), pl.ds(low + piece * (count // 2), count // 2), :]
 
-        offsets = (0, -1, 1, 2)
         held = {}
         state = {}
+        far = {}
 
         def along_two(d, src=None):
             i = turn(one, d, n)
@@ -106,42 +116,60 @@
             state["down"] = send(own, at(one, two), one_down)
             along_two(0, own)
 
-        def step_one():
+        def from_below():
             state["up"].wait_recv()
             i = turn(one, -1, n)
             state["far_up"] = send(at(i, two, 0), at(i, two, 0), one_up)
             along_two(-1)
+
+        def from_above():
             state["down"].wait_recv()
             i = turn(one, 1, n)
             state["far_down"] = send(at(i, two, 1), at(i, two, 1), one_down)
             along_two(1)
 
-        def step_two():
+        def from_far():
             state["far_up"].wait_recv()
             state["far_down"].wait_recv()
             along_two(2)
 
-        far = {}
-
-        def step_three(d):
-            up, down = held[d]
-            i = turn(one, d, n)
-            up.wait_recv()
-            j = turn(two, -1, n)
-            first = send(at(i, j, 0), at(i, j, 0), two_up)
-            down.wait_recv()
-            j = turn(two, 1, n)
-            far[d] = (first, send(at(i, j, 1), at(i, j, 1), two_down))
-
-        def step_four():
-            for d in offsets:
+        def across(d):
+            def run():
+                up, down = held[d]
+                i = turn(one, d, n)
+                up.wait_recv()
+                j = turn(two, -1, n)
+                first = send(at(i, j, 0), at(i, j, 0), two_up)
+                down.wait_recv()
+                j = turn(two, 1, n)
+                far[d] = (first, send(at(i, j, 1), at(i, j, 1), two_down))
+
+            return run
+
+        def last(d):
+            def run():
                 for copy in far[d]:
                     copy.wait_recv()
 
-        return start, step_one, step_two, step_three, step_four
-
-    fit_a = fit_gather(0, FIRST_ROWS, True)
-    fit_b = fit_gather(FIRST_ROWS, COLS - FIRST_ROWS, False)
+            return run
+
+        return [start, from_below, from_above, from_far] + [across(d) for d in (0, -1, 1, 2)] + [
+            last(d) for d in (0, -1, 1, 2)
+        ]
+
+    pieces = [fit_gather(*piece) for piece in PIECES]
+    fit_done = set()
+
+    def fit_stage(stages):
+        for stage in stages:
+            for number, piece in enumerate(pieces):
+                if (stage, number) not in fit_done:
+                    fit_done.add((stage, number))
+                    piece[stage]()
+
+    def hook(name):
+        return lambda: fit_stage(PLAN.get(name, ()))
+
     own_fit = pltpu.make_async_copy(fitted, fit_all.at[col], own_sem)
 
     def listed():
@@ -154,6 +182,8 @@
         return jnp.where(own == k, 0.0, fock[own, k])
 
     def prepare():
+        for load in loads[1:]:
+            load.wait()
         domains = dom[...].astype(F32)
         columns = jnp.concatenate([domains, jnp.zeros((ROWS - NORB, DOM), F32)], axis=0).T
         lanes = lax.broadcasted_iota(jnp.int32, (DOM, ROWS), 1)
@@ -189,31 +219,41 @@
         return jnp.broadcast_to(row_level, (ROWS, COLS)) + jnp.broadcast_to(col_level, (COLS, ROWS)).T
 
     def panel_gather(at, between, arrived):
-        ends = [lambda: None] * 8 if between is None else between
-        pair = send(at(y, zl), at(y, zl), z_pair)
-        ups = [send(at(y, zl), at(y, zl), y_up)]
-        downs = [send(at(y, zl), at(y, zl), y_down)]
-        ends[0]()
-        pair.wait_recv()
-        ups.append(send(at(y, 1 - zl), at(y, 1 - zl), y_up))
-        downs.append(send(at(y, 1 - zl), at(y, 1 - zl), y_down))
+        parts = range(2)
+        streams = [(zl, i) for i in parts] + [(1 - zl, i) for i in parts]
+        pairs_in = [send(at(y, *at_), at(y, *at_), z_pair) for at_ in streams[:2]]
+        ups = [send(at(y, *at_), at(y, *at_), y_up) for at_ in streams[:2]]
+        downs = [send(at(y, *at_), at(y, *at_), y_down) for at_ in streams[:2]]
+        between[0]()
+        for copy, at_ in zip(pairs_in, streams[2:]):
+            copy.wait_recv()
+            ups.append(send(at(y, *at_), at(y, *at_), y_up))
+            downs.append(send(at(y, *at_), at(y, *at_), y_down))
         arrived(y, None)
         for distance in (1, 2, 3):
             below, above = turn(y, -distance, NY), turn(y, distance, NY)
-            for p, place in enumerate((zl, 1 - zl)):
-                ups[p].wait_recv()
-                if distance < 3 or p == 0:
-                    ups[p] = send(at(below, place), at(below, place), y_up)
-                downs[p].wait_recv()
-                if distance < 3 or p == 1:
-                    downs[p] = send(at(above, place), at(above, place), y_down)
-                ends[distance * 2 - 1 + p]()
+            for n, at_ in enumerate(streams):
+                ups[n].wait_recv()
+                if distance < 3 or n < 2:
+                    ups[n] = send(at(below, *at_), at(below, *at_), y_up)
+                downs[n].wait_recv()
+                if distance < 3 or n >= 2:
+                    downs[n] = send(at(above, *at_), at(above, *at_), y_down)
+                if n % 2 == 1:
+                    between[distance * 2 - 1 + n // 2]()
             arrived(below, distance)
             arrived(above, distance)
-        ups[0].wait_recv()
-        downs[1].wait_recv()
+        for n in range(4):
+            (ups if n < 2 else downs)[n].wait_recv()
         arrived(turn(y, 4, NY), 4)
-        ends[7]()
+        between[7]()
+
+    def two(f, g):
+        def run():
+            f()
+            g()
+
+        return run
 
     def iteration(t, current, first):
         rounded = current.astype(BF16)
@@ -261,11 +301,12 @@
             pass
 
         panel_gather(
-            lambda k, p: lefts.at[k, p],
-            (first, nothing, right_far, nothing, right_one, nothing, right_two, nothing),
+            lambda k, p, i: lefts.at[k, p, pl.ds(i * (ROWS // 2), ROWS // 2)],
+            tuple(two(f, hook((t, i))) for i, f in enumerate((first, nothing, right_far, nothing, right_one, nothing, right_two, nothing))),
             left_add,
         )
         sib_copy = send(left_part.at[t, 1 - core], left_sib.at[t], sibling)
+        hook((t, 8))()
         right_copy[0].wait_recv()
         right_term = right_part[t, half] + right_recv[t]
         sib_copy.wait_recv()
@@ -273,24 +314,15 @@
         return weight * ((left_term + right_term - exch[...].astype(F32)) / acc[:ROWS, :COLS])
 
     def start_fitted():
-        fit_a[0]()
-        fit_b[0]()
+        fit_stage(PLAN['start'])
         own_fit.start()
         acc[:ROWS, :COLS] = prepare()
 
-    def fit_one():
-        fit_b[1]()
-        fit_a[1]()
-
-    def fit_two():
-        fit_b[2]()
-        fit_a[2]()
-
     weight = listed()
+    loads[0].wait()
     current = iteration(0, amps[...], start_fitted)
-    fit_one()
+    hook((0, 9))()
     current = iteration(1, current, lambda: None)
-    fit_two()
 
     mir_sites = sites[0]
     sites[0] += 2
@@ -313,6 +345,7 @@
         def _():
             mir_recv[t] = mir_send[t]
 
+    hook((2, 0))()
     for t in range(2):
 
         @pl.when(jnp.logical_not(mine[t]))
@@ -336,25 +369,16 @@
         blocks = sym_all.at[k, core]
         sib_copies.append((k, send(blocks, blocks, sibling)))
 
-    def fit_three(*offsets):
-        def run():
-            for d in offsets:
-                fit_b[3](d)
-                fit_a[3](d)
-
-        return run
-
     def nothing():
         pass
 
     panel_gather(
-        lambda k, p: sym_all.at[k, core, p],
-        (nothing, nothing, fit_three(0), nothing, fit_three(-1), nothing, fit_three(1), fit_three(2)),
+        lambda k, p, i: sym_all.at[k, core, p, pl.ds(i * ROWS, ROWS)],
+        tuple(hook((3, i)) for i in range(8)),
         forward,
     )
     own_fit.wait()
-    fit_b[4]()
-    fit_a[4]()
+    fit_stage(range(12))
     acc[...] = jnp.zeros(acc.shape, F32)
     for k, copy in sib_copies:
         copy.wait_recv()
@@ -385,7 +409,7 @@
             jax.ShapeDtypeStruct((ROWS, COLS), F32),
             jax.ShapeDtypeStruct((COLS, width), BF16),
         ),
-        in_specs=[vmem, vmem, hbm, vmem, smem, vmem, smem],
+        in_specs=[hbm, hbm, hbm, hbm, smem, hbm, smem],
         out_specs=(vmem, vmem),
         scratch_shapes=[
             pltpu.VMEM((NX * NZ, COLS, width), BF16),
@@ -402,12 +426,17 @@
             pltpu.VMEM((2, ROWS, ROWS), F32),
             pltpu.VMEM((NY, 2, 2, COLS, ROWS), BF16),
             pltpu.VMEM((COLS, width), F32),
+            pltpu.VMEM((ROWS, COLS), F32),
+            pltpu.VMEM((ROWS, COLS), BF16),
+            pltpu.VMEM((pao_energy.shape[0] // ROWS, ROWS), F32),
+            pltpu.VMEM((NORB, DOM), jnp.int32),
             pltpu.SemaphoreType.DMA((MAX_COPIES,)),
             pltpu.SemaphoreType.DMA((MAX_COPIES,)),
             pltpu.SemaphoreType.DMA,
+            pltpu.SemaphoreType.DMA((4,)),
         ],
         compiler_params=pltpu.CompilerParams(
-            collective_id=0, has_side_effects=True, vmem_limit_bytes=48 * 1024 * 1024
+            collective_id=0, has_side_effects=True, vmem_limit_bytes=60 * 1024 * 1024
         ),
         cost_estimate=pl.CostEstimate(flops=2_000_000_000, bytes_accessed=20_000_000, transcendentals=0),
     )(

time: 151 us -> 128 us (0.85); the launches traced: 149 us -> 128 us
  Pallas kernels: 142 us -> 124 us
  local copies, waits for them, and re-layouts: 6.91 us -> 3.33 us
    pallas_call x1, Pallas kernels: 142 us -> 124 us  [body(): pl.pallas_call(kernel, out_shape=(jax.ShapeDtypeStruct((ROWS, COLS), F32)...]
    unnamed x16 -> x2, local copies, waits for them, and re-layouts: 6.91 us -> 3.33 us
where the time goes in v3:
time: 128 us
  Pallas kernels  124 us (97%)
  local copies, waits for them, and re-layouts  3.33 us (3%)
    pallas_call x1, Pallas kernels, body(): pl.pallas_call(kernel, out_shape=(jax.ShapeDtypeStruct((ROWS, COLS), F32)...  124 us
    unnamed x2, local copies, waits for them, and re-layouts  3.33 us

profile of v3, /device:TPU:1, one launch (start us, length us, event | category | flops | bytes accessed | tf_op | source)
XLA Modules:
  0.0 128.0 jit_solution(2888313327192399427)
XLA Ops:
  0.6 124.0 %shard_map.86 = (f32[128,256]{1,0:T(8,128)}, bf16[256,768]{1,0:T(8,128)(2,1)}) custom-call(f32[128,256]{1,0:T(8,128)} %amps_hbm.1, bf16[128,256]{1,0:T(8,128)(2,1)} %exch_hbm.1, bf16[256,768]{1,0:T(8,128)(2,1)} %fitted.1, f32[16,128]{1,0:T(8,128)} %bitcast.2, f32[8,8]{1,0:T(8,128)} %fock.1, s32[8,512]{1,0:T(8,128)} %dom_hbm.1, s32[2,36]{1,0:T(2,128)} %bitcast.3), custom_call_target="tpu_custom_call" | custom-call | flops 2000000000 | bytes 20000000 | tf_op jit(solution)/shard_map/pallas_call | solution.py:406
  124.7 1.6 %copy.11 = f32[128,256]{1,0:T(8,128)} copy(f32[128,256]{1,0:T(8,128)} %get-tuple-element.4) | data formatting | bytes 262144
  126.2 1.8 %copy.12 = bf16[256,768]{1,0:T(8,128)(2,1)} copy(bf16[256,768]{1,0:T(8,128)(2,1)} %get-tuple-element.5) | data formatting | bytes 786432

commit v4 on v3

--- a/solution.py
+++ b/solution.py
@@ -9,10 +9,21 @@
 MESH = pl.DeviceIdType.MESH
 F32 = jnp.float32
 BF16 = jnp.bfloat16
-ROWS, COLS, DOM, NORB = 128, 256, 512, 8
+ROWS, HALF, COLS, DOM, NORB = 128, 64, 256, 512, 8
 NY, NX, NZ = 8, 4, 4
-PIECES = ((0, 256, True),)
-PLAN = {'start': [0], (0, 6): [1, 2], (0, 8): [4], (1, 2): [3], (1, 4): [5], (1, 8): [6], (2, 0): [7], (3, 4): [8, 9, 10, 11]}
+PIECE = 128
+PLAN = {
+    (0, 0): (('own', 0), ('x', 0, 0)),
+    (0, 2): (('own', 1),),
+    (0, 4): (('x', 0, 1),),
+    (0, 7): (('near', 0), ('near', 1)),
+    (0, 8): (('turn', 0, 0), ('turn', 0, 1)),
+    (0, 9): (('x', -1, 0), ('x', -1, 1)),
+    (1, 4): (('far', 0), ('far', 1)),
+    (1, 6): (('turn', -1, 0), ('turn', -1, 1), ('x', 1, 0), ('x', 1, 1)),
+    (2, 0): (('x', 2, 0), ('x', 2, 1), ('turn', 1, 0), ('turn', 1, 1)),
+    (3, 4): (('turn', 2, 0), ('turn', 2, 1)),
+}
 MAX_COPIES = 256
 
 
@@ -23,7 +34,7 @@
 def kernel(
     amps_hbm, exch_hbm, fitted, energy_hbm, fock, dom_hbm, pairs,
     sym_out, gamma_out,
-    fit_all, left_all, right_all, left_part, left_sib, right_part, right_recv,
+    fit_all, left_all, right_send, right_all, left_part, left_sib, right_part, right_recv,
     left_hot, right_hot, levels, mir_send, mir_recv, sym_all, acc, amps, exch, energy, dom,
     send_sems, recv_sems, own_sem, load_sems,
 ):
@@ -43,6 +54,7 @@
     x_up, x_down = device(x_=turn(x, 1, NX)), device(x_=turn(x, -1, NX))
     z_up, z_down = device(zh_=turn(zh, 1, NZ)), device(zh_=turn(zh, -1, NZ))
     z_far = device(zh_=turn(zh, 2, NZ))
+    z_other = device(zh_=(1 - b2) * 2 + 1 - half)
     z_pair = device(zl_=1 - zl)
     sibling = device(core_=1 - core)
     half_pair = device(zh_=b2 * 2 + 1 - half)
@@ -86,89 +98,57 @@
         sent.append(copy)
         return copy
 
-    def fit_gather(low, count, first_is_z):
-        if first_is_z:
-            one, two, n = zh, x, NZ
-            one_up, one_down, two_up, two_down = z_up, z_down, x_up, x_down
-            slot = lambda i, j: j * 4 + i
-        else:
-            one, two, n = x, zh, NX
-            one_up, one_down, two_up, two_down = x_up, x_down, z_up, z_down
-            slot = lambda i, j: i * 4 + j
-
-        def at(i, j, piece=None):
-            if piece is None:
-                return fit_all.at[slot(i, j), pl.ds(low, count), :]
-            return fit_all.at[slot(i, j), pl.ds(low + piece * (count // 2), count // 2), :]
-
-        held = {}
-        state = {}
-        far = {}
-
-        def along_two(d, src=None):
-            i = turn(one, d, n)
-            src = at(i, two) if src is None else src
-            held[d] = (send(src, at(i, two), two_up), send(src, at(i, two), two_down))
-
-        def start():
-            own = fitted.at[pl.ds(low, count), :]
-            state["up"] = send(own, at(one, two), one_up)
-            state["down"] = send(own, at(one, two), one_down)
-            along_two(0, own)
-
-        def from_below():
-            state["up"].wait_recv()
-            i = turn(one, -1, n)
-            state["far_up"] = send(at(i, two, 0), at(i, two, 0), one_up)
-            along_two(-1)
-
-        def from_above():
-            state["down"].wait_recv()
-            i = turn(one, 1, n)
-            state["far_down"] = send(at(i, two, 1), at(i, two, 1), one_down)
-            along_two(1)
-
-        def from_far():
-            state["far_up"].wait_recv()
-            state["far_down"].wait_recv()
-            along_two(2)
-
-        def across(d):
-            def run():
-                up, down = held[d]
-                i = turn(one, d, n)
-                up.wait_recv()
-                j = turn(two, -1, n)
-                first = send(at(i, j, 0), at(i, j, 0), two_up)
-                down.wait_recv()
-                j = turn(two, 1, n)
-                far[d] = (first, send(at(i, j, 1), at(i, j, 1), two_down))
-
-            return run
-
-        def last(d):
-            def run():
-                for copy in far[d]:
-                    copy.wait_recv()
-
-            return run
-
-        return [start, from_below, from_above, from_far] + [across(d) for d in (0, -1, 1, 2)] + [
-            last(d) for d in (0, -1, 1, 2)
-        ]
-
-    pieces = [fit_gather(*piece) for piece in PIECES]
-    fit_done = set()
-
-    def fit_stage(stages):
-        for stage in stages:
-            for number, piece in enumerate(pieces):
-                if (stage, number) not in fit_done:
-                    fit_done.add((stage, number))
-                    piece[stage]()
-
-    def hook(name):
-        return lambda: fit_stage(PLAN.get(name, ()))
+    z_slot = {0: zh, -1: turn(zh, -1, NZ), 1: turn(zh, 1, NZ), 2: turn(zh, 2, NZ)}
+    fit_sent = {}
+
+    def fit_at(d, x_place, n, share=None):
+        low, count = n * PIECE, PIECE
+        if share is not None:
+            low, count = low + share * (PIECE // 2), PIECE // 2
+        return fit_all.at[x_place * NZ + z_slot[d], pl.ds(low, count), :]
+
+    def fit_own_z(n):
+        own = fitted.at[pl.ds(n * PIECE, PIECE), :]
+        fit_sent["z", -1, n] = send(own, fit_at(0, x, n), z_up)
+        fit_sent["z", 1, n] = send(own, fit_at(0, x, n), z_down)
+
+    def fit_x(d, n):
+        src = fitted.at[pl.ds(n * PIECE, PIECE), :] if d == 0 else fit_at(d, x, n)
+        fit_sent["x", d, n] = [send(src, fit_at(d, x, n), to) for to in (x_up, x_down)]
+
+    def fit_near_z(n):
+        for d, share, to in ((-1, 0, z_up), (1, 1, z_down)):
+            fit_sent["z", d, n].wait_recv()
+            fit_sent["far", share, n] = send(fit_at(d, x, n, share), fit_at(d, x, n, share), to)
+
+    def fit_far_z(n):
+        for share in range(2):
+            fit_sent["far", share, n].wait_recv()
+
+    def fit_turn_x(d, n):
+        up, down = fit_sent["x", d, n]
+        last = []
+        for copy, by, share, to in ((up, -1, 0, x_up), (down, 1, 1, x_down)):
+            copy.wait_recv()
+            block = fit_at(d, turn(x, by, NX), n, share)
+            last.append(send(block, block, to))
+        fit_sent["last", d, n] = last
+
+    def fit_last(d, n):
+        for copy in fit_sent["last", d, n]:
+            copy.wait_recv()
+
+    actions = {
+        "own": fit_own_z, "near": fit_near_z, "far": fit_far_z, "x": fit_x, "turn": fit_turn_x,
+        "last": fit_last,
+    }
+
+    def hook(*place):
+        def run():
+            for step in PLAN.get(place, ()):
+                actions[step[0]](*step[1:])
+
+        return run
 
     own_fit = pltpu.make_async_copy(fitted, fit_all.at[col], own_sem)
 
@@ -201,9 +181,7 @@
             ]
             picked = jnp.concatenate(picked, axis=1).astype(F32)
             left_hot[k] = jnp.where(own_rows == picked, 1.0, 0.0).astype(BF16)
-            levels[4] = columns[:, k : k + 1]
-            picked = levels[4, pl.ds(pl.multiple_of(half * COLS, COLS), COLS), :]
-            right_hot[k] = jnp.where(picked == own_cols, 1.0, 0.0).astype(BF16)
+            right_hot[k] = jnp.where(columns[:, k : k + 1] == own_cols, 1.0, 0.0).astype(BF16)
 
         def level_of(paos):
             found = jnp.zeros((paos.shape[0], ROWS), F32)
@@ -258,14 +236,21 @@
     def iteration(t, current, first):
         rounded = current.astype(BF16)
         left_all[t, y, zl] = rounded
-        right_all[t, orb] = rounded
+        right_send[t] = rounded.reshape(2, HALF, COLS)
+        right_all[t, orb, half] = right_send[t, half]
         lefts, rights = left_all.at[t], right_all.at[t]
         other = x * 2 + 1 - b2
-        far = send(rights.at[orb], rights.at[orb], z_far)
-        x_one = [send(rights.at[orb], rights.at[orb], to) for to in (x_up, x_down, x_far)]
+        sources = right_send.at[t]
+        z_copies = [
+            send(sources.at[1 - half], rights.at[orb, half], half_pair),
+            send(sources.at[half], rights.at[orb, half], z_far),
+            send(sources.at[1 - half], rights.at[orb, half], z_other),
+        ]
+        x_tos = (x_up, x_down, x_far)
+        x_one = [send(rights.at[orb, half], rights.at[orb, half], to) for to in x_tos]
         x_two = []
         left_part[t] = jnp.zeros((2, ROWS, COLS), F32)
-        right_part[t] = jnp.zeros((2, ROWS, COLS), F32)
+        right_part[t] = jnp.zeros((2, HALF, COLS), F32)
 
         def left_add(k, distance):
             if distance is not None:
@@ -274,55 +259,59 @@
                 left_part[t] += term.reshape(2, ROWS, COLS)
 
         def right_add(k):
-            term = jnp.dot(right_all[t, k], right_hot[k], preferred_element_type=F32)
-            term = term * off_diagonal(orb, k)
+            block = jnp.concatenate([right_all[t, k, 0], right_all[t, k, 1]], axis=1)
+            term = jnp.dot(block, right_hot[k], preferred_element_type=F32) * off_diagonal(orb, k)
             right_part[t, 0] += term[:, :COLS]
             right_part[t, 1] += term[:, COLS:]
 
         def right_far():
-            far.wait_recv()
-            x_two.extend(send(rights.at[other], rights.at[other], to) for to in (x_up, x_down, x_far))
+            for copy in z_copies:
+                copy.wait_recv()
+            for place in (rights.at[orb, 1 - half], rights.at[other]):
+                x_two.append([send(place, place, to) for to in x_tos])
 
         def right_one():
             right_add(other)
-            for copy, by in zip(x_one, (-1, 1, 2)):
-                copy.wait_recv()
+            for n, by in enumerate((-1, 1, 2)):
+                x_one[n].wait_recv()
+                x_two[0][n].wait_recv()
                 right_add(turn(x, by, NX) * 2 + b2)
 
         right_copy = []
 
         def right_two():
-            for copy, by in zip(x_two, (-1, 1, 2)):
-                copy.wait_recv()
+            for n, by in enumerate((-1, 1, 2)):
+                x_two[1][n].wait_recv()
                 right_add(turn(x, by, NX) * 2 + 1 - b2)
-            right_copy.append(send(right_part.at[t, 1 - half], right_recv.at[t], half_pair))
+            right_recv[t, half] = right_part[t, half]
+            right_copy.append(send(right_part.at[t, 1 - half], right_recv.at[t, half], half_pair))
 
         def nothing():
             pass
 
         panel_gather(
             lambda k, p, i: lefts.at[k, p, pl.ds(i * (ROWS // 2), ROWS // 2)],
-            tuple(two(f, hook((t, i))) for i, f in enumerate((first, nothing, right_far, nothing, right_one, nothing, right_two, nothing))),
+            tuple(two(f, hook(t, i) if i else nothing) for i, f in enumerate((first, nothing, right_far, nothing, right_one, nothing, right_two, nothing))),
             left_add,
         )
         sib_copy = send(left_part.at[t, 1 - core], left_sib.at[t], sibling)
-        hook((t, 8))()
+        hook(t, 8)()
         right_copy[0].wait_recv()
-        right_term = right_part[t, half] + right_recv[t]
+        right_term = right_recv[t].reshape(ROWS, COLS)
         sib_copy.wait_recv()
         left_term = left_part[t, core] + left_sib[t]
         return weight * ((left_term + right_term - exch[...].astype(F32)) / acc[:ROWS, :COLS])
 
     def start_fitted():
-        fit_stage(PLAN['start'])
+        hook(0, 0)()
         own_fit.start()
         acc[:ROWS, :COLS] = prepare()
 
     weight = listed()
     loads[0].wait()
     current = iteration(0, amps[...], start_fitted)
-    hook((0, 9))()
-    current = iteration(1, current, lambda: None)
+    hook(0, 9)()
+    current = iteration(1, current, hook(1, 0))
 
     mir_sites = sites[0]
     sites[0] += 2
@@ -345,7 +334,7 @@
         def _():
             mir_recv[t] = mir_send[t]
 
-    hook((2, 0))()
+    hook(2, 0)()
     for t in range(2):
 
         @pl.when(jnp.logical_not(mine[t]))
@@ -374,11 +363,13 @@
 
     panel_gather(
         lambda k, p, i: sym_all.at[k, core, p, pl.ds(i * ROWS, ROWS)],
-        tuple(hook((3, i)) for i in range(8)),
+        tuple(hook(3, i) for i in range(8)),
         forward,
     )
     own_fit.wait()
-    fit_stage(range(12))
+    for d in (0, -1, 1, 2):
+        for n in range(COLS // PIECE):
+            fit_last(d, n)
     acc[...] = jnp.zeros(acc.shape, F32)
     for k, copy in sib_copies:
         copy.wait_recv()
@@ -414,14 +405,15 @@
         scratch_shapes=[
             pltpu.VMEM((NX * NZ, COLS, width), BF16),
             pltpu.VMEM((ITERS, NORB, 2, ROWS, COLS), BF16),
-            pltpu.VMEM((ITERS, NORB, ROWS, COLS), BF16),
+            pltpu.VMEM((ITERS, 2, HALF, COLS), BF16),
+            pltpu.VMEM((ITERS, NORB, 2, HALF, COLS), BF16),
             pltpu.VMEM((ITERS, 2, ROWS, COLS), F32),
             pltpu.VMEM((ITERS, ROWS, COLS), F32),
-            pltpu.VMEM((ITERS, 2, ROWS, COLS), F32),
-            pltpu.VMEM((ITERS, ROWS, COLS), F32),
+            pltpu.VMEM((ITERS, 2, HALF, COLS), F32),
+            pltpu.VMEM((ITERS, 2, HALF, COLS), F32),
             pltpu.VMEM((NORB, 2 * ROWS, 2 * ROWS), BF16),
-            pltpu.VMEM((NORB, COLS, DOM), BF16),
-            pltpu.VMEM((5, DOM, 1), F32),
+            pltpu.VMEM((NORB, DOM, DOM), BF16),
+            pltpu.VMEM((4, DOM, 1), F32),
             pltpu.VMEM((2, ROWS, ROWS), F32),
             pltpu.VMEM((2, ROWS, ROWS), F32),
             pltpu.VMEM((NY, 2, 2, COLS, ROWS), BF16),

time: 128 us -> 122 us (0.953)
  Pallas kernels: 124 us -> 117 us
    pallas_call x1, Pallas kernels: 124 us -> 117 us  [body(): pl.pallas_call(kernel, out_shape=(jax.ShapeDtypeStruct((ROWS, COLS), F32)...]
where the time goes in v4:
time: 122 us; the launch traced here: 121 us
  Pallas kernels  117 us (96%)
  local copies, waits for them, and re-layouts  3.33 us (3%)
    pallas_call x1, Pallas kernels, body(): pl.pallas_call(kernel, out_shape=(jax.ShapeDtypeStruct((ROWS, COLS), F32)...  117 us
    unnamed x2, local copies, waits for them, and re-layouts  3.33 us

profile of v4, /device:TPU:1, one launch (start us, length us, event | category | flops | bytes accessed | tf_op | source)
XLA Modules:
  0.0 121.1 jit_solution(18432445286419446631)
XLA Ops:
  0.6 117.2 %shard_map.86 = (f32[128,256]{1,0:T(8,128)}, bf16[256,768]{1,0:T(8,128)(2,1)}) custom-call(f32[128,256]{1,0:T(8,128)} %amps_hbm.1, bf16[128,256]{1,0:T(8,128)(2,1)} %exch_hbm.1, bf16[256,768]{1,0:T(8,128)(2,1)} %fitted.1, f32[16,128]{1,0:T(8,128)} %bitcast.2, f32[8,8]{1,0:T(8,128)} %fock.1, s32[8,512]{1,0:T(8,128)} %dom_hbm.1, s32[2,36]{1,0:T(2,128)} %bitcast.3), custom_call_target="tpu_custom_call" | custom-call | flops 2000000000 | bytes 20000000 | tf_op jit(solution)/shard_map/pallas_call | solution.py:397
  117.8 1.6 %copy.11 = f32[128,256]{1,0:T(8,128)} copy(f32[128,256]{1,0:T(8,128)} %get-tuple-element.4) | data formatting | bytes 262144
  119.4 1.8 %copy.12 = bf16[256,768]{1,0:T(8,128)(2,1)} copy(bf16[256,768]{1,0:T(8,128)(2,1)} %get-tuple-element.5) | data formatting | bytes 786432

commit v5 on v4

--- a/solution.py
+++ b/solution.py
@@ -11,18 +11,21 @@
 BF16 = jnp.bfloat16
 ROWS, HALF, COLS, DOM, NORB = 128, 64, 256, 512, 8
 NY, NX, NZ = 8, 4, 4
-PIECE = 128
+PIECES = ((0, 128, 'z'), (128, 96, 'z'), (224, 32, 'x'))
 PLAN = {
-    (0, 0): (('own', 0), ('x', 0, 0)),
+    (0, 0): (('own', 0), ('trail', 0, 0)),
     (0, 2): (('own', 1),),
-    (0, 4): (('x', 0, 1),),
-    (0, 7): (('near', 0), ('near', 1)),
+    (0, 4): (('trail', 0, 1), ('own', 2)),
+    (0, 7): (('near', 0), ('near', 1), ('trail', 0, 2)),
     (0, 8): (('turn', 0, 0), ('turn', 0, 1)),
-    (0, 9): (('x', -1, 0), ('x', -1, 1)),
-    (1, 4): (('far', 0), ('far', 1)),
-    (1, 6): (('turn', -1, 0), ('turn', -1, 1), ('x', 1, 0), ('x', 1, 1)),
-    (2, 0): (('x', 2, 0), ('x', 2, 1), ('turn', 1, 0), ('turn', 1, 1)),
-    (3, 4): (('turn', 2, 0), ('turn', 2, 1)),
+    (0, 9): (('trail', -1, 0), ('trail', -1, 1), ('near', 2)),
+    (1, 2): (('trail', -1, 2), ('trail', 1, 2)),
+    (1, 4): (('far', 0), ('far', 1), ('far', 2)),
+    (1, 5): (('trail', 1, 0), ('trail', 1, 1)),
+    (1, 7): (('turn', 0, 2), ('trail', 2, 2)),
+    (1, 8): (('turn', -1, 0), ('turn', -1, 1)),
+    (2, 0): (('trail', 2, 0), ('trail', 2, 1), ('turn', 1, 0), ('turn', 1, 1), ('turn', -1, 2), ('turn', 1, 2)),
+    (3, 4): (('turn', 2, 0), ('turn', 2, 1), ('turn', 2, 2)),
 }
 MAX_COPIES = 256
 
@@ -35,7 +38,7 @@
     amps_hbm, exch_hbm, fitted, energy_hbm, fock, dom_hbm, pairs,
     sym_out, gamma_out,
     fit_all, left_all, right_send, right_all, left_part, left_sib, right_part, right_recv,
-    left_hot, right_hot, levels, mir_send, mir_recv, sym_all, acc, amps, exch, energy, dom,
+    left_hot, right_hot, levels, mir_send, mir_relay, mir_recv, sym_all, acc, amps, exch, energy, dom,
     send_sems, recv_sems, own_sem, load_sems,
 ):
     row = lax.axis_index("row")
@@ -59,9 +62,11 @@
     sibling = device(core_=1 - core)
     half_pair = device(zh_=b2 * 2 + 1 - half)
     diagonal = row // 2 == col
-    mirror = [
-        {"row": col * 2 + t, "col": row // 2} for t in range(2)
+    relays = [
+        {"row": col * 2 + c, "col": turn(row // 8, k, NX) * 4 + lax.rem(row // 2, 4)}
+        for k in range(NX) for c in range(2)
     ]
+    x_shares = [device(x_=turn(x, k, NX)) for k in range(1, NX)]
     mine = [jnp.logical_and(diagonal, core == t) for t in range(2)]
 
     loads = [
@@ -74,15 +79,15 @@
         load.start()
     barrier = pltpu.get_barrier_semaphore()
     partners = [y_up, y_down, x_up, x_down, x_far, z_up, z_down, z_far, z_pair, sibling]
-    for partner in partners:
+    for partner in partners + relays[2:]:
         pl.semaphore_signal(barrier, inc=1, device_id=partner, device_id_type=MESH)
-    for t in range(2):
-
-        @pl.when(jnp.logical_not(mine[t]))
+    for c in range(2):
+
+        @pl.when(jnp.logical_not(mine[c]))
         def _():
-            pl.semaphore_signal(barrier, inc=1, device_id=mirror[t], device_id_type=MESH)
-
-    pl.semaphore_wait(barrier, len(partners) + 2 - diagonal.astype(jnp.int32))
+            pl.semaphore_signal(barrier, inc=1, device_id=relays[c], device_id_type=MESH)
+
+    pl.semaphore_wait(barrier, len(partners) + 2 * NX - diagonal.astype(jnp.int32))
 
     sent = []
     sites = [0]
@@ -98,39 +103,47 @@
         sent.append(copy)
         return copy
 
-    z_slot = {0: zh, -1: turn(zh, -1, NZ), 1: turn(zh, 1, NZ), 2: turn(zh, 2, NZ)}
     fit_sent = {}
 
-    def fit_at(d, x_place, n, share=None):
-        low, count = n * PIECE, PIECE
+    def fit_ways(n, lead):
+        along_z = (PIECES[n][2] == "z") == lead
+        return (z_up, z_down) if along_z else (x_up, x_down)
+
+    def fit_at(n, d, by=0, share=None):
+        low, count, lead = PIECES[n]
         if share is not None:
-            low, count = low + share * (PIECE // 2), PIECE // 2
-        return fit_all.at[x_place * NZ + z_slot[d], pl.ds(low, count), :]
-
-    def fit_own_z(n):
-        own = fitted.at[pl.ds(n * PIECE, PIECE), :]
-        fit_sent["z", -1, n] = send(own, fit_at(0, x, n), z_up)
-        fit_sent["z", 1, n] = send(own, fit_at(0, x, n), z_down)
-
-    def fit_x(d, n):
-        src = fitted.at[pl.ds(n * PIECE, PIECE), :] if d == 0 else fit_at(d, x, n)
-        fit_sent["x", d, n] = [send(src, fit_at(d, x, n), to) for to in (x_up, x_down)]
-
-    def fit_near_z(n):
-        for d, share, to in ((-1, 0, z_up), (1, 1, z_down)):
-            fit_sent["z", d, n].wait_recv()
-            fit_sent["far", share, n] = send(fit_at(d, x, n, share), fit_at(d, x, n, share), to)
-
-    def fit_far_z(n):
+            low, count = low + share * (count // 2), count // 2
+        if lead == "x":
+            d, by = by, d
+        return fit_all.at[turn(x, by, NX) * NZ + turn(zh, d, NZ), pl.ds(low, count), :]
+
+    def fit_mine(n):
+        return fitted.at[pl.ds(PIECES[n][0], PIECES[n][1]), :]
+
+    def fit_own(n):
+        up, down = fit_ways(n, True)
+        fit_sent["lead", -1, n] = send(fit_mine(n), fit_at(n, 0), up)
+        fit_sent["lead", 1, n] = send(fit_mine(n), fit_at(n, 0), down)
+
+    def fit_trail(d, n):
+        src = fit_mine(n) if d == 0 else fit_at(n, d)
+        fit_sent["trail", d, n] = [send(src, fit_at(n, d), to) for to in fit_ways(n, False)]
+
+    def fit_near(n):
+        for d, share, to in zip((-1, 1), (0, 1), fit_ways(n, True)):
+            fit_sent["lead", d, n].wait_recv()
+            block = fit_at(n, d, 0, share)
+            fit_sent["far", share, n] = send(block, block, to)
+
+    def fit_far(n):
         for share in range(2):
             fit_sent["far", share, n].wait_recv()
 
-    def fit_turn_x(d, n):
-        up, down = fit_sent["x", d, n]
+    def fit_turn(d, n):
         last = []
-        for copy, by, share, to in ((up, -1, 0, x_up), (down, 1, 1, x_down)):
+        for copy, by, share, to in zip(fit_sent["trail", d, n], (-1, 1), (0, 1), fit_ways(n, False)):
             copy.wait_recv()
-            block = fit_at(d, turn(x, by, NX), n, share)
+            block = fit_at(n, d, by, share)
             last.append(send(block, block, to))
         fit_sent["last", d, n] = last
 
@@ -139,8 +152,7 @@
             copy.wait_recv()
 
     actions = {
-        "own": fit_own_z, "near": fit_near_z, "far": fit_far_z, "x": fit_x, "turn": fit_turn_x,
-        "last": fit_last,
+        "own": fit_own, "near": fit_near, "far": fit_far, "trail": fit_trail, "turn": fit_turn,
     }
 
     def hook(*place):
@@ -314,36 +326,49 @@
     current = iteration(1, current, hook(1, 0))
 
     mir_sites = sites[0]
-    sites[0] += 2
-    mir_copies = []
+    sites[0] += 2 * NX
+    mir_rows = ROWS // NX
     for t in range(2):
-        mir_send[t] = current[:, t * ROWS : (t + 1) * ROWS].T
-        mir_copies.append(
-            pltpu.make_async_remote_copy(
-                src_ref=mir_send.at[t], dst_ref=mir_recv.at[core],
-                send_sem=send_sems.at[mir_sites + t], recv_sem=recv_sems.at[mir_sites + core],
-                device_id=mirror[t], device_id_type=MESH,
-            )
+        tile = current[:, t * ROWS : (t + 1) * ROWS].T
+        for k in range(NX):
+            mir_send[k, t] = tile[k * mir_rows : (k + 1) * mir_rows]
+    shared = [
+        send(mir_send.at[k], mir_relay.at[k], x_shares[k - 1]) for k in range(1, NX)
+    ]
+
+    def mirror_copy(k, t):
+        source = mir_send if k == 0 else mir_relay
+        return pltpu.make_async_remote_copy(
+            src_ref=source.at[k, t], dst_ref=mir_recv.at[core, pl.ds(k * mir_rows, mir_rows)],
+            send_sem=send_sems.at[mir_sites + k * 2 + t],
+            recv_sem=recv_sems.at[mir_sites + core * NX + k],
+            device_id={"row": (turn(x, -k, NX) * 4 + zh) * 2 + t, "col": row // 2}, device_id_type=MESH,
         )
+
+    for t in range(2):
 
         @pl.when(jnp.logical_not(mine[t]))
         def _():
-            mir_copies[t].start()
+            mirror_copy(0, t).start()
 
         @pl.when(mine[t])
         def _():
-            mir_recv[t] = mir_send[t]
-
+            pltpu.make_async_copy(
+                mir_send.at[0, t], mir_recv.at[core, pl.ds(0, mir_rows)],
+                recv_sems.at[mir_sites + core * NX],
+            ).start()
+
+    for k in range(1, NX):
+        shared[k - 1].wait_recv()
+        for t in range(2):
+            copy = mirror_copy(k, t)
+            copy.start()
+            sent.append(copy)
     hook(2, 0)()
-    for t in range(2):
-
-        @pl.when(jnp.logical_not(mine[t]))
-        def _():
-            pltpu.make_async_remote_copy(
-                src_ref=mir_send.at[t], dst_ref=mir_recv.at[t],
-                send_sem=send_sems.at[mir_sites + t], recv_sem=recv_sems.at[mir_sites + t],
-                device_id=mirror[t], device_id_type=MESH,
-            ).wait_recv()
+    for c in range(2):
+        for k in range(NX):
+            place = mir_recv.at[c, pl.ds(k * mir_rows, mir_rows)]
+            pltpu.make_async_copy(place, place, recv_sems.at[mir_sites + c * NX + k]).wait()
 
     sym_halves = [
         0.5 * (current[:, t * ROWS : (t + 1) * ROWS] + mir_recv[t]) for t in range(2)
@@ -368,7 +393,7 @@
     )
     own_fit.wait()
     for d in (0, -1, 1, 2):
-        for n in range(COLS // PIECE):
+        for n in range(len(PIECES)):
             fit_last(d, n)
     acc[...] = jnp.zeros(acc.shape, F32)
     for k, copy in sib_copies:
@@ -386,7 +411,11 @@
 
         @pl.when(jnp.logical_not(mine[t]))
         def _():
-            mir_copies[t].wait_send()
+            mirror_copy(0, t).wait_send()
+
+
+def in_hbm(array):
+    return pltpu.with_memory_space_constraint(array, pltpu.HBM)
 
 
 def body(start_amps, exchange_ints, fitted_ints, pao_energy, occ_fock, domains, pair_list):
@@ -414,7 +443,8 @@
             pltpu.VMEM((NORB, 2 * ROWS, 2 * ROWS), BF16),
             pltpu.VMEM((NORB, DOM, DOM), BF16),
             pltpu.VMEM((4, DOM, 1), F32),
-            pltpu.VMEM((2, ROWS, ROWS), F32),
+            pltpu.VMEM((NX, 2, ROWS // NX, ROWS), F32),
+            pltpu.VMEM((NX, 2, ROWS // NX, ROWS), F32),
             pltpu.VMEM((2, ROWS, ROWS), F32),
             pltpu.VMEM((NY, 2, 2, COLS, ROWS), BF16),
             pltpu.VMEM((COLS, width), F32),
@@ -428,11 +458,12 @@
             pltpu.SemaphoreType.DMA((4,)),
         ],
         compiler_params=pltpu.CompilerParams(
-            collective_id=0, has_side_effects=True, vmem_limit_bytes=60 * 1024 * 1024
+            collective_id=0, has_side_effects=True, vmem_limit_bytes=48 * 1024 * 1024
         ),
         cost_estimate=pl.CostEstimate(flops=2_000_000_000, bytes_accessed=20_000_000, transcendentals=0),
     )(
-        start_amps, exchange_ints, fitted_ints, pao_energy.reshape(-1, ROWS), occ_fock, domains, pair_list.T
+        in_hbm(start_amps), in_hbm(exchange_ints), in_hbm(fitted_ints), in_hbm(pao_energy.reshape(-1, ROWS)),
+        in_hbm(occ_fock), in_hbm(domains), in_hbm(pair_list.T),
     )
 
 

time: 122 us -> 113 us (0.926)
  Pallas kernels: 117 us -> 111 us
  local copies, waits for them, and re-layouts: 3.33 us -> 1.4 us
    pallas_call x1, Pallas kernels: 117 us -> 111 us  [body(): pl.pallas_call(kernel, out_shape=(jax.ShapeDtypeStruct((ROWS, COLS), F32)...]
    unnamed x2, local copies, waits for them, and re-layouts: 3.33 us -> 1.4 us
where the time goes in v5:
time: 113 us
  Pallas kernels  111 us (98%)
  local copies, waits for them, and re-layouts  1.4 us (1%)
    pallas_call x1, Pallas kernels, body(): pl.pallas_call(kernel, out_shape=(jax.ShapeDtypeStruct((ROWS, COLS), F32)...  111 us

profile of v5, /device:TPU:1, one launch (start us, length us, event | category | flops | bytes accessed | tf_op | source)
XLA Modules:
  0.0 112.5 jit_solution(2976131479676618939)
XLA Ops:
  0.6 110.5 %shard_map.86 = (f32[128,256]{1,0:T(8,128)S(1)}, bf16[256,768]{1,0:T(8,128)(2,1)S(1)}) custom-call(f32[128,256]{1,0:T(8,128)} %amps_hbm.1, bf16[128,256]{1,0:T(8,128)(2,1)} %exch_hbm.1, bf16[256,768]{1,0:T(8,128)(2,1)} %fitted.1, f32[16,128]{1,0:T(8,128)} %bitcast.2, f32[8,8]{1,0:T(8,128)} %fock.1, s32[8,512]{1,0:T(8,128)} %dom_hbm.1, s32[2,36]{1,0:T(2,128)} %bitcast.3), custom_call_target="tpu_custom_call" | custom-call | flops 2000000000 | bytes 20000000 | tf_op jit(solution)/shard_map/pallas_call | solution.py:426
  111.1 0.7 copy.11
  111.8 0.7 copy.12

commit v6 on v5

--- a/solution.py
+++ b/solution.py
@@ -16,14 +16,12 @@
     (0, 0): (('own', 0), ('trail', 0, 0)),
     (0, 2): (('own', 1),),
     (0, 4): (('trail', 0, 1), ('own', 2)),
-    (0, 7): (('near', 0), ('near', 1), ('trail', 0, 2)),
-    (0, 8): (('turn', 0, 0), ('turn', 0, 1)),
-    (0, 9): (('trail', -1, 0), ('trail', -1, 1), ('near', 2)),
+    (0, 8): (('near', 0), ('near', 1), ('trail', 0, 2), ('turn', 0, 0), ('turn', 0, 1)),
+    (1, 0): (('trail', -1, 0), ('trail', -1, 1), ('near', 2)),
     (1, 2): (('trail', -1, 2), ('trail', 1, 2)),
     (1, 4): (('far', 0), ('far', 1), ('far', 2)),
     (1, 5): (('trail', 1, 0), ('trail', 1, 1)),
-    (1, 7): (('turn', 0, 2), ('trail', 2, 2)),
-    (1, 8): (('turn', -1, 0), ('turn', -1, 1)),
+    (1, 8): (('turn', 0, 2), ('trail', 2, 2), ('turn', -1, 0), ('turn', -1, 1)),
     (2, 0): (('trail', 2, 0), ('trail', 2, 1), ('turn', 1, 0), ('turn', 1, 1), ('turn', -1, 2), ('turn', 1, 2)),
     (3, 4): (('turn', 2, 0), ('turn', 2, 1), ('turn', 2, 2)),
 }
@@ -312,14 +310,16 @@
         right_term = right_recv[t].reshape(ROWS, COLS)
         sib_copy.wait_recv()
         left_term = left_part[t, core] + left_sib[t]
-        return weight * ((left_term + right_term - exch[...].astype(F32)) / acc[:ROWS, :COLS])
+        return weight[0] * ((left_term + right_term - exch[...].astype(F32)) / acc[:ROWS, :COLS])
+
+    weight = []
 
     def start_fitted():
         hook(0, 0)()
         own_fit.start()
+        weight.append(listed())
         acc[:ROWS, :COLS] = prepare()
 
-    weight = listed()
     loads[0].wait()
     current = iteration(0, amps[...], start_fitted)
     hook(0, 9)()

time: 113 us -> 111 us (0.982)
  Pallas kernels: 111 us -> 108 us
    pallas_call x1, Pallas kernels: 111 us -> 108 us  [body(): pl.pallas_call(kernel, out_shape=(jax.ShapeDtypeStruct((ROWS, COLS), F32)...]
where the time goes in v6:
time: 111 us; the launch traced here: 110 us
  Pallas kernels  108 us (97%)
  local copies, waits for them, and re-layouts  1.4 us (1%)
    pallas_call x1, Pallas kernels, body(): pl.pallas_call(kernel, out_shape=(jax.ShapeDtypeStruct((ROWS, COLS), F32)...  108 us

profile of v6, /device:TPU:1, one launch (start us, length us, event | category | flops | bytes accessed | tf_op | source)
XLA Modules:
  0.0 110.4 jit_solution(16575125206012587567)
XLA Ops:
  0.6 108.3 %shard_map.86 = (f32[128,256]{1,0:T(8,128)S(1)}, bf16[256,768]{1,0:T(8,128)(2,1)S(1)}) custom-call(f32[128,256]{1,0:T(8,128)} %amps_hbm.1, bf16[128,256]{1,0:T(8,128)(2,1)} %exch_hbm.1, bf16[256,768]{1,0:T(8,128)(2,1)} %fitted.1, f32[16,128]{1,0:T(8,128)} %bitcast.2, f32[8,8]{1,0:T(8,128)} %fock.1, s32[8,512]{1,0:T(8,128)} %dom_hbm.1, s32[2,36]{1,0:T(2,128)} %bitcast.3), custom_call_target="tpu_custom_call" | custom-call | flops 2000000000 | bytes 20000000 | tf_op jit(solution)/shard_map/pallas_call | solution.py:426
  109.0 0.7 copy.11
  109.6 0.7 copy.12
